TPU v7x, 512 devices: a whole 4x8x8 slice. The times are simulated.
512 devices in a mesh: dp: 8 (over y), row: 16 (over z, x_hi), lon: 4 (over x_lo, core).
Axes of the slice: x: 4 (x_hi: 2, x_lo: 2; x = x_hi * 2 + x_lo), y: 8, z: 8, core: 2. Of those that a mesh axis runs over, the one named last changes fastest.
Arguments:
- features: bfloat16 [8, 96, 144, 2048], P('dp', 'row', 'lon'), may hold values from -6 to 6
- depthwise_kernels: bfloat16 [2, 3, 3, 2048], replicated, may hold values from -2 to 2
- point_weights: bfloat16 [2, 2048, 256], replicated, may hold values from -0.125 to 0.125
- proj_weight: bfloat16 [512, 256], replicated, may hold values from -0.25 to 0.25
- class_weight: bfloat16 [256, 3], replicated, may hold values from -1.25 to 1.25
- labels: int32 [8, 96, 144], P('dp', 'row', 'lon'), may hold values from 0 to 2
Outputs:
- input_grad: bfloat16 [8, 96, 144, 2048], P('dp', 'row', 'lon')
- point_grad: float32 [2, 2048, 256], P(None, ('row', 'lon'), 'dp')
All inputs are finite; a program needn't handle non-finite values.
Results may differ from a plain program's by a relative error of at most 0.025.
Values may be sent and summed in bfloat16 or wider, within the bound.
A program may use at most 128 MiB of HBM per device.

v0:
```python
import math

import jax
import jax.numpy as jnp
from jax import lax
from jax.sharding import PartitionSpec as P

DILATION_INNER = 12
DILATION_OUTER = 36


loss_scale = 32.0


def with_halo(block, sides, width):
    for axis, dim in sides:
        count = lax.axis_size(axis)
        forward = [(i, i + 1) for i in range(count - 1)]
        forward.append((count - 1, 0))
        backward = [(target, source) for source, target in forward]
        low = lax.ppermute(
            lax.slice_in_dim(block, block.shape[dim] - width, None, axis=dim), axis, forward
        )
        high = lax.ppermute(lax.slice_in_dim(block, 0, width, axis=dim), axis, backward)
        block = jnp.concatenate([low, block, high], axis=dim)
    return block


def passed_along(block, axis, distance):
    devices = range(lax.axis_size(axis))
    route = [(i - distance, i) for i in devices if i - distance in devices]
    return lax.ppermute(block, axis, route)


def silu_slope(value):
    sigma = jax.nn.sigmoid(value)
    return sigma * (1.0 + value * (1.0 - sigma))


def longitude_margin(array_in, rim_width):
    return with_halo(array_in, (("lon", 2),), rim_width)


def row_partials(wrapped_input, kernel, rim_width, dilation, column_count, direction):
    partials = []
    for row_tap in range(3):
        total_sum = None
        for col_tap in range(3):
            begin_col = rim_width + direction * (col_tap - 1) * dilation
            piece = wrapped_input[:, :, begin_col : begin_col + column_count, :].astype(
                jnp.float32
            ) * kernel[row_tap, col_tap].astype(jnp.float32)
            total_sum = piece if total_sum is None else total_sum + piece
        partials.append(total_sum.astype(jnp.bfloat16))
    return partials


def shifted_rows(partials, dilation, rows_dev, direction):
    device_hops = dilation // rows_dev
    total_sum = partials[1].astype(jnp.float32)
    for row_tap in (0, 2):
        offset = direction * (row_tap - 1)
        arrived = passed_along(partials[row_tap], "row", -offset * device_hops)
        total_sum = total_sum + arrived.astype(jnp.float32)
    return total_sum


def shards(features, depthwise_kernels, point_weights, proj_weight, class_weight, labels):
    dilation_list = (DILATION_INNER, DILATION_OUTER)
    rows_dev = features.shape[1]
    column_count = features.shape[2]
    channels = features.shape[3]
    pixels = rows_dev * column_count
    wrapped_input = longitude_margin(features, DILATION_OUTER)
    depth_list = []
    for branch_index in range(2):
        partials = row_partials(
            wrapped_input,
            depthwise_kernels[branch_index],
            DILATION_OUTER,
            dilation_list[branch_index],
            column_count,
            1,
        )
        depth_list.append(
            shifted_rows(partials, dilation_list[branch_index], rows_dev, 1).astype(jnp.bfloat16)
        )
    depth_all = jnp.concatenate(depth_list, axis=0)
    flat_depth = depth_all.reshape(2, pixels, channels)
    point_pre = [
        jnp.dot(
            flat_depth[branch_index],
            point_weights[branch_index],
            preferred_element_type=jnp.float32,
        )
        for branch_index in range(2)
    ]
    joined = jnp.concatenate(
        [jax.nn.silu(point_pre[branch_index]).astype(jnp.bfloat16) for branch_index in range(2)],
        axis=1,
    )
    proj_pre = jnp.dot(joined, proj_weight, preferred_element_type=jnp.float32)
    projected = jax.nn.silu(proj_pre).astype(jnp.bfloat16)
    logits = jnp.dot(projected, class_weight, preferred_element_type=jnp.float32)
    label_flat = labels.reshape(pixels)
    onehot = (
        label_flat[:, None] == jnp.arange(class_weight.shape[1], dtype=jnp.int32)[None, :]
    ).astype(jnp.float32)
    grad_logits = (loss_scale * (jax.nn.softmax(logits, axis=1) - onehot)).astype(jnp.bfloat16)
    grad_proj = (
        jnp.dot(grad_logits, class_weight.T, preferred_element_type=jnp.float32)
        * silu_slope(proj_pre)
    ).astype(jnp.bfloat16)
    grad_joined = jnp.dot(grad_proj, proj_weight.T, preferred_element_type=jnp.float32)
    out_width = point_weights.shape[2]
    point_terms = []
    grad_depths = []
    for branch_index in range(2):
        grad_act = (
            grad_joined[:, branch_index * out_width : (branch_index + 1) * out_width]
            * silu_slope(point_pre[branch_index])
        ).astype(jnp.bfloat16)
        point_terms.append(
            jnp.dot(flat_depth[branch_index].T, grad_act, preferred_element_type=jnp.float32)
        )
        grad_depths.append(
            jnp.dot(
                grad_act, point_weights[branch_index].T, preferred_element_type=jnp.float32
            ).astype(jnp.bfloat16)
        )
    grad_depth = jnp.stack(grad_depths).reshape(2, rows_dev, column_count, channels)
    total_grad = None
    for branch_index in range(2):
        wrapped_input = longitude_margin(
            grad_depth[branch_index : branch_index + 1], dilation_list[branch_index]
        )
        partials = row_partials(
            wrapped_input,
            depthwise_kernels[branch_index],
            dilation_list[branch_index],
            dilation_list[branch_index],
            column_count,
            -1,
        )
        contrib = shifted_rows(partials, dilation_list[branch_index], rows_dev, -1)
        total_grad = contrib if total_grad is None else total_grad + contrib
    input_grad = total_grad.astype(jnp.bfloat16)
    pixel_count = (
        lax.axis_size("dp")
        * lax.axis_size("row")
        * lax.axis_size("lon")
        * features.shape[0]
        * pixels
    )
    grad_scale = 1.0 / math.sqrt(pixel_count)
    spatial = lax.psum_scatter(
        jnp.stack(point_terms), ("row", "lon"), scatter_dimension=1, tiled=True
    )
    point_grad = (
        lax.psum_scatter(
            spatial.astype(jnp.bfloat16), "dp", scatter_dimension=2, tiled=True
        ).astype(jnp.float32)
        * grad_scale
    )
    return (input_grad, point_grad)


def solution(mesh):
    placed = (P("dp", "row", "lon", None), P(), P(), P(), P(), P("dp", "row", "lon"))
    return jax.shard_map(
        shards,
        mesh=mesh,
        in_specs=placed,
        out_specs=(P("dp", "row", "lon", None), P(None, ("row", "lon"), "dp")),
        check_vma=False,
    )
```

profile of v0, /device:TPU:1, one launch (start us, length us, event | category | flops | bytes accessed | tf_op | source)
XLA Modules:
  0.0 388.5 jit_solution(10480310830744447887)
XLA Ops:
  7.2 4.6 %collective-permute-start = (bf16[1,6,36,2048]{3,2,1,0:T(8,128)(2,1)}, bf16[1,6,36,2048]{3,2,1,0:T(8,128)(2,1)S(1)}, u32[]{:S(2)}, u32[]{:S(2)}) collective-permute-start(bf16[1,6,36,2048]{3,2,1,0:T(8,128)(2,1)} %param.6), channel_id=1, source_target_pairs={{0,1},{1,2},{2,3},{3,0},{4,5},{5,6},{6,7},{7,4},{8,9},{9,10},{10,1... | collective-permute-start | bytes 2654216 | tf_op jit(solution)/shard_map/ppermute | solution.py:21
  11.9 6.2 %collective-permute-start.1 = (bf16[1,6,36,2048]{3,2,1,0:T(8,128)(2,1)}, bf16[1,6,36,2048]{3,2,1,0:T(8,128)(2,1)S(1)}, u32[]{:S(2)}, u32[]{:S(2)}) collective-permute-start(bf16[1,6,36,2048]{3,2,1,0:T(8,128)(2,1)} %param.6), channel_id=1, source_target_pairs={{1,0},{2,1},{3,2},{0,3},{5,4},{6,5},{7,6},{4,7},{9,8},{10,9},{11,1... | collective-permute-start | bytes 2654216 | tf_op jit(solution)/shard_map/ppermute | solution.py:24
  18.1 1.1 fusion.75
  19.4 6.2 %collective-permute-done = bf16[1,6,36,2048]{3,2,1,0:T(8,128)(2,1)S(1)} collective-permute-done((bf16[1,6,36,2048]{3,2,1,0:T(8,128)(2,1)}, bf16[1,6,36,2048]{3,2,1,0:T(8,128)(2,1)S(1)}, u32[]{:S(2)}, u32[]{:S(2)}) %collective-permute-start) | collective-permute-done | bytes 884768 | tf_op jit(solution)/shard_map/ppermute | solution.py:21
  25.6 11.0 %collective-permute-done.1 = bf16[1,6,36,2048]{3,2,1,0:T(8,128)(2,1)S(1)} collective-permute-done((bf16[1,6,36,2048]{3,2,1,0:T(8,128)(2,1)}, bf16[1,6,36,2048]{3,2,1,0:T(8,128)(2,1)S(1)}, u32[]{:S(2)}, u32[]{:S(2)}) %collective-permute-start.1) | collective-permute-done | bytes 884768 | tf_op jit(solution)/shard_map/ppermute | solution.py:24
  36.6 4.6 %fusion.5 = (bf16[1,6,36,2048]{3,2,1,0:T(8,128)(2,1)}, bf16[1,6,36,2048]{3,2,1,0:T(8,128)(2,1)}, bf16[1,6,36,2048]{3,2,1,0:T(8,128)(2,1)}) fusion(bf16[1,6,36,2048]{3,2,1,0:T(8,128)(2,1)} %param.6, f32[2048]{0:T(1024)S(1)} %bitcast.73, f32[2048]{0:T(1024)S(1)} %bitcast.75, f32[2048]{0:T(1024)S(1)} %bitcast.77, ...), kind=kLoop, calls=%fused_computation.46 | loop fusion | flops 12828672 | bytes 5382144 | tf_op jit(solution)/shard_map/convert_element_type | solution.py:54
  41.2 2.7 collective-permute-start.2
  43.9 8.9 %collective-permute-start.4 = (bf16[1,6,36,2048]{3,2,1,0:T(8,128)(2,1)}, bf16[1,6,36,2048]{3,2,1,0:T(8,128)(2,1)}, u32[]{:S(2)}, u32[]{:S(2)}) collective-permute-start(bf16[1,6,36,2048]{3,2,1,0:T(8,128)(2,1)} %get-tuple-element.7), channel_id=1, source_target_pairs={{0,24},{4,28},{8,32},{12,36},{16,40},{20,44},{24,48},{28,52},{32,5... | collective-permute-start | bytes 2654216 | tf_op jit(solution)/shard_map/ppermute | solution.py:32
  52.7 1.3 collective-permute-start.5
  54.0 1.7 fusion.8
  55.7 1.3 collective-permute-start.3
  57.1 5.7 %collective-permute-done.2 = bf16[1,6,36,2048]{3,2,1,0:T(8,128)(2,1)} collective-permute-done((bf16[1,6,36,2048]{3,2,1,0:T(8,128)(2,1)}, bf16[1,6,36,2048]{3,2,1,0:T(8,128)(2,1)}, u32[]{:S(2)}, u32[]{:S(2)}) %collective-permute-start.2) | collective-permute-done | bytes 884768 | tf_op jit(solution)/shard_map/ppermute | solution.py:32
  62.8 21.1 %collective-permute-done.4 = bf16[1,6,36,2048]{3,2,1,0:T(8,128)(2,1)} collective-permute-done((bf16[1,6,36,2048]{3,2,1,0:T(8,128)(2,1)}, bf16[1,6,36,2048]{3,2,1,0:T(8,128)(2,1)}, u32[]{:S(2)}, u32[]{:S(2)}) %collective-permute-start.4) | collective-permute-done | bytes 884768 | tf_op jit(solution)/shard_map/ppermute | solution.py:32
  83.9 16.6 %collective-permute-done.5 = bf16[1,6,36,2048]{3,2,1,0:T(8,128)(2,1)} collective-permute-done((bf16[1,6,36,2048]{3,2,1,0:T(8,128)(2,1)}, bf16[1,6,36,2048]{3,2,1,0:T(8,128)(2,1)}, u32[]{:S(2)}, u32[]{:S(2)}) %collective-permute-start.5) | collective-permute-done | bytes 884768 | tf_op jit(solution)/shard_map/ppermute | solution.py:32
  100.6 0.2 collective-permute-done.3
  100.8 4.7 %add_convert_fusion.2 = (bf16[1,6,36,2048]{3,2,1,0:T(8,128)(2,1)}, bf16[1,6,36,2048]{3,2,1,0:T(8,128)(2,1)}) fusion(bf16[1,6,36,2048]{3,2,1,0:T(8,128)(2,1)} %collective-permute-done.3, bf16[1,6,36,2048]{3,2,1,0:T(8,128)(2,1)} %collective-permute-done.2, bf16[1,6,36,2048]{3,2,1,0:T(8,128)(2,1)S(1)} %copy-done.1, f32[2048]{0:T(1024)S(1)} %bitcast.87, ...), kind=kLoop, calls=%fused_computation.79 | loop fusion | flops 15482880 | bytes 8011776 | tf_op jit(solution)/shard_map/convert_element_type | solution.py:86
  105.5 1.4 squeeze.16
  107.2 1.8 multiply_convert_fusion.1
  109.1 0.4 multiply_convert_fusion.2
  109.5 0.2 fusion.50
  109.8 0.2 fusion.76
  110.0 0.4 fusion.37
  110.4 0.2 fusion.49
  110.6 0.5 convolution_bitcast_fusion
  111.1 0.5 convolution_bitcast_fusion.1
  111.6 2.2 pad_maximum_fusion
  113.9 1.7 convolution_convert_fusion
  115.8 3.8 collective-permute-start.10
  119.6 2.2 collective-permute-start.11
  121.8 2.6 convolution_convert_fusion.1
  124.4 1.3 slice.163
  125.8 2.2 collective-permute-start.6
  127.9 3.4 collective-permute-start.7
  131.4 16.4 %collective-permute-done.6 = bf16[1,6,12,2048]{3,2,1,0:T(8,128)(2,1)S(1)} collective-permute-done((bf16[1,6,12,2048]{3,2,1,0:T(8,128)(2,1)S(1)}, bf16[1,6,12,2048]{3,2,1,0:T(8,128)(2,1)S(1)}, u32[]{:S(2)}, u32[]{:S(2)}) %collective-permute-start.6) | collective-permute-done | bytes 294944 | tf_op jit(solution)/shard_map/ppermute | solution.py:24
  147.7 2.4 collective-permute-done.7
  150.1 2.3 fusion.23
  152.5 1.3 collective-permute-start.8
  153.8 26.9 %collective-permute-start.9 = (bf16[1,6,36,2048]{3,2,1,0:T(8,128)(2,1)}, bf16[1,6,36,2048]{3,2,1,0:T(8,128)(2,1)}, u32[]{:S(2)}, u32[]{:S(2)}) collective-permute-start(bf16[1,6,36,2048]{3,2,1,0:T(8,128)(2,1)} %get-tuple-element.10), channel_id=1, source_target_pairs={{0,8},{4,12},{8,16},{12,20},{16,24},{20,28},{24,32},{28,36},{32,40... | collective-permute-start | bytes 2654216 | tf_op jit(solution)/shard_map/ppermute | solution.py:32
  180.6 3.4 fusion.32
  184.0 1.3 collective-permute-start.12
  185.3 26.3 %collective-permute-start.13 = (bf16[1,6,36,2048]{3,2,1,0:T(8,128)(2,1)}, bf16[1,6,36,2048]{3,2,1,0:T(8,128)(2,1)}, u32[]{:S(2)}, u32[]{:S(2)}) collective-permute-start(bf16[1,6,36,2048]{3,2,1,0:T(8,128)(2,1)} %get-tuple-element.3), channel_id=1, source_target_pairs={{0,24},{4,28},{8,32},{12,36},{16,40},{20,44},{24,48},{28,52},{32,5... | collective-permute-start | bytes 2654216 | tf_op jit(solution)/shard_map/ppermute | solution.py:32
  211.6 129.1 %reduce-scatter.5.cloned.1.call-done = f32[2,32,256]{2,1,0:T(8,128)} async-done(((f32[2,2048,256]{2,1,0:T(8,128)}), f32[2,32,256]{2,1,0:T(8,128)}) %reduce-scatter.5.cloned.1.call-update) | async-done | bytes 65552 | tf_op jit(solution)/shard_map/reduce_scatter | solution.py:156
  340.8 0.8 convert_element_type.489
  341.7 0.7 reshape.261
  342.6 5.0 %add_convert_fusion = bf16[1,6,36,2048]{3,2,1,0:T(8,128)(2,1)} fusion(bf16[1,6,36,2048]{3,2,1,0:T(8,128)(2,1)} %collective-permute-done.13, bf16[1,6,36,2048]{3,2,1,0:T(8,128)(2,1)} %collective-permute-done.12, bf16[1,6,36,2048]{3,2,1,0:T(8,128)(2,1)} %collective-permute-done.9, bf16[1,6,36,2048]{3,2,1,0:T(8,128)(2,1)} %collective-permute-done.8, ...), kind=kLoop, calls=%fused_computation.77 | loop fusion | flops 15925248 | bytes 8601600 | tf_op jit(solution)/shard_map/convert_element_type | solution.py:147
  347.6 32.6 %reduce-scatter.7.cloned.1.call-done = bf16[32,64]{1,0:T(8,128)(2,1)} async-done(((bf16[256,64]{1,0:T(8,128)(2,1)}), bf16[32,64]{1,0:T(8,128)(2,1)}) %reduce-scatter.7.cloned.1.call-update) | async-done | bytes 4112
  380.1 0.8 reshape.262
  381.0 0.6 convert_multiply_fusion.36
  (37 shorter events, 1.3 us)
Async XLA Ops:
  7.2 102.4 %copy-start = (bf16[512,256]{1,0:T(8,128)(2,1)S(1)}, bf16[512,256]{1,0:T(8,128)(2,1)}, u32[]{:S(2)}) copy-start(bf16[512,256]{1,0:T(8,128)(2,1)} %param.9) | copy-start | bytes 786436
  7.2 333.6 %reduce-scatter.5.cloned.1.call-start = ((), (), s32[]{:S(2)}) async-start(), calls=%async_computation.2 | async-start | bytes 4259840 | tf_op jit(solution)/shard_map/reduce_scatter | solution.py:156
  7.2 18.3 %collective-permute-start = (bf16[1,6,36,2048]{3,2,1,0:T(8,128)(2,1)}, bf16[1,6,36,2048]{3,2,1,0:T(8,128)(2,1)S(1)}, u32[]{:S(2)}, u32[]{:S(2)}) collective-permute-start(bf16[1,6,36,2048]{3,2,1,0:T(8,128)(2,1)} %param.6), channel_id=1, source_target_pairs={{0,1},{1,2},{2,3},{3,0},{4,5},{5,6},{6,7},{7,4},{8,9},{9,10},{10,1... | collective-permute-start | bytes 2654216 | tf_op jit(solution)/shard_map/ppermute | solution.py:21
  11.9 24.7 %collective-permute-start.1 = (bf16[1,6,36,2048]{3,2,1,0:T(8,128)(2,1)}, bf16[1,6,36,2048]{3,2,1,0:T(8,128)(2,1)S(1)}, u32[]{:S(2)}, u32[]{:S(2)}) collective-permute-start(bf16[1,6,36,2048]{3,2,1,0:T(8,128)(2,1)} %param.6), channel_id=1, source_target_pairs={{1,0},{2,1},{3,2},{0,3},{5,4},{6,5},{7,6},{4,7},{9,8},{10,9},{11,1... | collective-permute-start | bytes 2654216 | tf_op jit(solution)/shard_map/ppermute | solution.py:24
  36.6 17.4 %copy-start.1 = (bf16[1,6,36,2048]{3,2,1,0:T(8,128)(2,1)S(1)}, bf16[1,6,36,2048]{3,2,1,0:T(8,128)(2,1)}, u32[]{:S(2)}) copy-start(bf16[1,6,36,2048]{3,2,1,0:T(8,128)(2,1)} %param.6) | copy-start | bytes 2654212
  41.2 21.7 %collective-permute-start.2 = (bf16[1,6,36,2048]{3,2,1,0:T(8,128)(2,1)}, bf16[1,6,36,2048]{3,2,1,0:T(8,128)(2,1)}, u32[]{:S(2)}, u32[]{:S(2)}) collective-permute-start(bf16[1,6,36,2048]{3,2,1,0:T(8,128)(2,1)} %get-tuple-element.6), channel_id=1, source_target_pairs={{0,8},{4,12},{8,16},{12,20},{16,24},{20,28},{24,32},{28,36},{32,40... | collective-permute-start | bytes 2654216 | tf_op jit(solution)/shard_map/ppermute | solution.py:32
  43.9 40.1 %collective-permute-start.4 = (bf16[1,6,36,2048]{3,2,1,0:T(8,128)(2,1)}, bf16[1,6,36,2048]{3,2,1,0:T(8,128)(2,1)}, u32[]{:S(2)}, u32[]{:S(2)}) collective-permute-start(bf16[1,6,36,2048]{3,2,1,0:T(8,128)(2,1)} %get-tuple-element.7), channel_id=1, source_target_pairs={{0,24},{4,28},{8,32},{12,36},{16,40},{20,44},{24,48},{28,52},{32,5... | collective-permute-start | bytes 2654216 | tf_op jit(solution)/shard_map/ppermute | solution.py:32
  52.7 47.9 %collective-permute-start.5 = (bf16[1,6,36,2048]{3,2,1,0:T(8,128)(2,1)}, bf16[1,6,36,2048]{3,2,1,0:T(8,128)(2,1)}, u32[]{:S(2)}, u32[]{:S(2)}) collective-permute-start(bf16[1,6,36,2048]{3,2,1,0:T(8,128)(2,1)} %get-tuple-element.8), channel_id=1, source_target_pairs={{24,0},{28,4},{32,8},{36,12},{40,16},{44,20},{48,24},{52,28},{56,3... | collective-permute-start | bytes 2654216 | tf_op jit(solution)/shard_map/ppermute | solution.py:32
  54.0 3.0 copy-start.6
  55.7 45.1 %collective-permute-start.3 = (bf16[1,6,36,2048]{3,2,1,0:T(8,128)(2,1)}, bf16[1,6,36,2048]{3,2,1,0:T(8,128)(2,1)}, u32[]{:S(2)}, u32[]{:S(2)}) collective-permute-start(bf16[1,6,36,2048]{3,2,1,0:T(8,128)(2,1)} %fusion.8), channel_id=1, source_target_pairs={{8,0},{12,4},{16,8},{20,12},{24,16},{28,20},{32,24},{36,28},{40,32... | collective-permute-start | bytes 2654216 | tf_op jit(solution)/shard_map/ppermute | solution.py:32
  105.5 1.5 copy-start.2
  107.2 1.9 copy-start.3
  109.1 0.7 copy-start.7
  113.9 266.3 %reduce-scatter.7.cloned.1.call-start = ((), (), s32[]{:S(2)}) async-start(), calls=%async_computation.3 | async-start | bytes 73728
  115.8 64.8 %collective-permute-start.10 = (bf16[1,6,36,2048]{3,2,1,0:T(8,128)(2,1)S(1)}, bf16[1,6,36,2048]{3,2,1,0:T(8,128)(2,1)S(1)}, u32[]{:S(2)}, u32[]{:S(2)}) collective-permute-start(bf16[1,6,36,2048]{3,2,1,0:T(8,128)(2,1)S(1)} %slice.169), channel_id=1, source_target_pairs={{1,0},{2,1},{3,2},{0,3},{5,4},{6,5},{7,6},{4,7},{9,8},{10,9},{11,1... | collective-permute-start | bytes 2654216 | tf_op jit(solution)/shard_map/ppermute | solution.py:24
  119.6 61.0 %collective-permute-start.11 = (bf16[1,6,36,2048]{3,2,1,0:T(8,128)(2,1)S(1)}, bf16[1,6,36,2048]{3,2,1,0:T(8,128)(2,1)}, u32[]{:S(2)}, u32[]{:S(2)}) collective-permute-start(bf16[1,6,36,2048]{3,2,1,0:T(8,128)(2,1)S(1)} %slice.169), channel_id=1, source_target_pairs={{0,1},{1,2},{2,3},{3,0},{4,5},{5,6},{6,7},{7,4},{8,9},{9,10},{10,1... | collective-permute-start | bytes 2654216 | tf_op jit(solution)/shard_map/ppermute | solution.py:21
  125.8 21.9 %collective-permute-start.6 = (bf16[1,6,12,2048]{3,2,1,0:T(8,128)(2,1)S(1)}, bf16[1,6,12,2048]{3,2,1,0:T(8,128)(2,1)S(1)}, u32[]{:S(2)}, u32[]{:S(2)}) collective-permute-start(bf16[1,6,12,2048]{3,2,1,0:T(8,128)(2,1)S(1)} %get-tuple-element.11), channel_id=1, source_target_pairs={{1,0},{2,1},{3,2},{0,3},{5,4},{6,5},{7,6},{4,7},{9,8},{10,9},{11,1... | collective-permute-start | bytes 884744 | tf_op jit(solution)/shard_map/ppermute | solution.py:24
  127.9 22.2 %collective-permute-start.7 = (bf16[1,6,12,2048]{3,2,1,0:T(8,128)(2,1)S(1)}, bf16[1,6,12,2048]{3,2,1,0:T(8,128)(2,1)S(1)}, u32[]{:S(2)}, u32[]{:S(2)}) collective-permute-start(bf16[1,6,12,2048]{3,2,1,0:T(8,128)(2,1)S(1)} %get-tuple-element.12), channel_id=1, source_target_pairs={{0,1},{1,2},{2,3},{3,0},{4,5},{5,6},{6,7},{7,4},{8,9},{9,10},{10,1... | collective-permute-start | bytes 884744 | tf_op jit(solution)/shard_map/ppermute | solution.py:21
  147.7 36.3 %copy-start.4 = (bf16[1,6,12,2048]{3,2,1,0:T(8,128)(2,1)}, bf16[1,6,12,2048]{3,2,1,0:T(8,128)(2,1)S(1)}, u32[]{:S(2)}) copy-start(bf16[1,6,12,2048]{3,2,1,0:T(8,128)(2,1)S(1)} %collective-permute-done.6) | copy-start | bytes 884740
  150.1 33.9 %copy-start.5 = (bf16[1,6,12,2048]{3,2,1,0:T(8,128)(2,1)}, bf16[1,6,12,2048]{3,2,1,0:T(8,128)(2,1)S(1)}, u32[]{:S(2)}) copy-start(bf16[1,6,12,2048]{3,2,1,0:T(8,128)(2,1)S(1)} %collective-permute-done.7) | copy-start | bytes 884740
  152.5 190.0 %collective-permute-start.8 = (bf16[1,6,36,2048]{3,2,1,0:T(8,128)(2,1)}, bf16[1,6,36,2048]{3,2,1,0:T(8,128)(2,1)}, u32[]{:S(2)}, u32[]{:S(2)}) collective-permute-start(bf16[1,6,36,2048]{3,2,1,0:T(8,128)(2,1)} %get-tuple-element.9), channel_id=1, source_target_pairs={{8,0},{12,4},{16,8},{20,12},{24,16},{28,20},{32,24},{36,28},{40,32... | collective-permute-start | bytes 2654216 | tf_op jit(solution)/shard_map/ppermute | solution.py:32
  153.8 188.8 %collective-permute-start.9 = (bf16[1,6,36,2048]{3,2,1,0:T(8,128)(2,1)}, bf16[1,6,36,2048]{3,2,1,0:T(8,128)(2,1)}, u32[]{:S(2)}, u32[]{:S(2)}) collective-permute-start(bf16[1,6,36,2048]{3,2,1,0:T(8,128)(2,1)} %get-tuple-element.10), channel_id=1, source_target_pairs={{0,8},{4,12},{8,16},{12,20},{16,24},{20,28},{24,32},{28,36},{32,40... | collective-permute-start | bytes 2654216 | tf_op jit(solution)/shard_map/ppermute | solution.py:32
  184.0 158.5 %collective-permute-start.12 = (bf16[1,6,36,2048]{3,2,1,0:T(8,128)(2,1)}, bf16[1,6,36,2048]{3,2,1,0:T(8,128)(2,1)}, u32[]{:S(2)}, u32[]{:S(2)}) collective-permute-start(bf16[1,6,36,2048]{3,2,1,0:T(8,128)(2,1)} %get-tuple-element.2), channel_id=1, source_target_pairs={{24,0},{28,4},{32,8},{36,12},{40,16},{44,20},{48,24},{52,28},{56,3... | collective-permute-start | bytes 2654216 | tf_op jit(solution)/shard_map/ppermute | solution.py:32
  185.3 157.2 %collective-permute-start.13 = (bf16[1,6,36,2048]{3,2,1,0:T(8,128)(2,1)}, bf16[1,6,36,2048]{3,2,1,0:T(8,128)(2,1)}, u32[]{:S(2)}, u32[]{:S(2)}) collective-permute-start(bf16[1,6,36,2048]{3,2,1,0:T(8,128)(2,1)} %get-tuple-element.3), channel_id=1, source_target_pairs={{0,24},{4,28},{8,32},{12,36},{16,40},{20,44},{24,48},{28,52},{32,5... | collective-permute-start | bytes 2654216 | tf_op jit(solution)/shard_map/ppermute | solution.py:32
Sparse Core Ops, SparseCore 0:
  114.0 226.7 reduce-scatter.4
  343.8 36.3 reduce-scatter.6
where the time goes:
time: 394 us; the launch traced here: 388 us
  waiting for transfers between devices  241 us (61%)
  starting transfers between devices  92.3 us (23%)
  other arithmetic  25.7 us (7%)
  between operations  14.3 us (4%)
  matrix products  8.44 us (2%)
  local copies, waits for them, and re-layouts  6.31 us (2%)
    reduce_scatter x1, waiting for transfers between devices, shards(): lax.psum_scatter(jnp.stack(point_terms), ('row', 'lon'), scatter_dimensio...  129 us
    ppermute x8, starting transfers between devices, passed_along(): return lax.ppermute(block, axis, route)  69.9 us
    ppermute x8, waiting for transfers between devices, passed_along(): return lax.ppermute(block, axis, route)  43.7 us
    unnamed x3, waiting for transfers between devices  32.6 us
    ppermute x3, waiting for transfers between devices, with_halo(): lax.ppermute(lax.slice_in_dim(block, 0, width, axis=dim), axis, backward)  27.4 us
    ppermute x3, starting transfers between devices, with_halo(): lax.ppermute(lax.slice_in_dim(block, 0, width, axis=dim), axis, backward)  12.1 us
    convert_element_type x4, other arithmetic, row_partials(): partials.append(total_sum.astype(jnp.bfloat16))  12 us
    ppermute x3, starting transfers between devices, with_halo(): lax.ppermute(lax.slice_in_dim(block, block.shape[dim] - width, None, axis...  10.2 us
  transfers between devices with their start and end apart: 16, of which 10 were waited for; matrix products, arithmetic and copies ran while one was open for 5% of the time, Pallas kernels for 0%

commit v1 on v0

v1 whole, which is shorter than its diff:
```python
import functools
import math

import jax
import jax.numpy as jnp
from jax import lax
from jax.experimental import pallas as pl
from jax.experimental.pallas import tpu as pltpu
from jax.sharding import PartitionSpec as P

DILATION_INNER = 12
DILATION_OUTER = 36
GROUP = DILATION_INNER
LOSS_SCALE = 32.0
MESH = pl.DeviceIdType.MESH
NN = (((1,), (0,)), ((), ()))
NT = (((1,), (1,)), ((), ()))
F32 = jnp.float32
BF16 = jnp.bfloat16


def dot(a, b, dims=NN):
    return lax.dot_general(a, b, dims, preferred_element_type=F32)


def slope(value, sigma):
    return sigma * (1.0 + value * (1.0 - sigma))


def kernel(
    size, hops, scale,
    x_ref, k_ref, pw_ref, proj_ref, cls_ref, lab_ref,
    ig_ref, pg_ref,
    kf_ref, kb_ref, cacc_ref,
    yso_ref, yro_ref, ysi_ref, yri_ref,
    cs_ref, cr_ref,
    g0_ref, g1_ref, gt_ref, igacc_ref,
    t_ref, rc_ref, s_ref, ry_ref, u0_ref, rz0_ref, rz1_ref, u1_ref, ry1_ref, v_ref, rx_ref,
    ss_y, rs_y, ss_c, rs_c, ss_gz, rs_gz, ss_gl, rs_gl,
    ss_core, rs_core, ss_ry, rs_ry, ss_rz, rs_rz, ss_rx, rs_rx,
):
    ndp, nrow, nlon = size
    nz = nrow // 2
    channels = x_ref.shape[1]
    outc = pw_ref.shape[2]
    gp = g0_ref.shape[2]
    pix = 3 * gp
    pix_pad = x_ref.shape[0]
    y = lax.axis_index("dp")
    row = lax.axis_index("row")
    lon = lax.axis_index("lon")
    z = row // 2
    xh = row % 2
    core = lon % 2
    member = xh * nlon + lon
    right = {"lon": (lon + 1) % nlon}
    left = {"lon": (lon + nlon - 1) % nlon}
    partner = {"lon": lon + 1 - 2 * core}

    def along(shift):
        return {"row": (row + shift + nrow) % nrow}

    def dp_peer(k):
        return (y + k) % ndp

    def z_peer(k):
        return (z + k) % nz

    def x_peer(k):
        other = (member + k) % (2 * nlon)
        return {"row": z * 2 + other // nlon, "lon": other % nlon}

    started = []

    def send(src, dst, ssem, rsem, device):
        copy = pltpu.make_async_remote_copy(
            src_ref=src, dst_ref=dst, send_sem=ssem, recv_sem=rsem,
            device_id=device, device_id_type=MESH,
        )
        copy.start()
        started.append(copy)
        return copy

    barrier = pltpu.get_barrier_semaphore()
    peers = [left, right]
    for shift in hops:
        peers += [along(shift), along(-shift)]
    peers += [{"dp": dp_peer(k)} for k in range(1, ndp)]
    peers += [{"row": z_peer(k) * 2 + xh} for k in range(1, nz)]
    peers += [x_peer(k) for k in range(1, 2 * nlon)]
    for peer in peers:
        pl.semaphore_signal(barrier, inc=1, device_id=peer, device_id_type=MESH)

    kf_ref[...] = k_ref[...].astype(F32)
    for t in range(18):
        kb_ref[t] = jnp.broadcast_to(kf_ref[t : t + 1, :], (16, channels)).astype(BF16)

    def taps(b, i):
        x = x_ref[:pix, :].reshape(pix // 16, 16, channels)
        out = []
        for j in (0, 2, 1):
            scaled = (x * kb_ref[b * 9 + i * 3 + j][None]).reshape(pix, channels)
            out.append(dot(scaled, pw_ref[b]))
        return out

    pl.semaphore_wait(barrier, len(peers))

    lon_copies = {}

    def outer_taps(i):
        y0, y2, y1 = taps(1, i)
        cacc_ref[3 + i] = y1
        yso_ref[i, 0] = y0.astype(BF16)
        yso_ref[i, 1] = y2.astype(BF16)
        lon_copies[1, i] = [
            send(yso_ref.at[i, 0], yro_ref.at[i, 0], ss_y.at[6 + 2 * i], rs_y.at[6 + 2 * i], right),
            send(yso_ref.at[i, 1], yro_ref.at[i, 1], ss_y.at[7 + 2 * i], rs_y.at[7 + 2 * i], left),
        ]

    def inner_taps(i):
        y0, y2, y1 = taps(0, i)
        ysi_ref[i, 0] = y0[2 * gp :].astype(BF16)
        ysi_ref[i, 1] = y2[:gp].astype(BF16)
        lon_copies[0, i] = [
            send(ysi_ref.at[i, 0], yri_ref.at[i, 0], ss_y.at[2 * i], rs_y.at[2 * i], right),
            send(ysi_ref.at[i, 1], yri_ref.at[i, 1], ss_y.at[2 * i + 1], rs_y.at[2 * i + 1], left),
        ]
        cacc_ref[i] = y1
        cacc_ref[i, gp:, :] += y0[: 2 * gp]
        cacc_ref[i, : 2 * gp, :] += y2[gp:]

    def columns_done(b, i):
        for copy in lon_copies[b, i]:
            copy.wait_recv()
        if b == 1:
            cacc_ref[3 + i] += yro_ref[i, 0].astype(F32) + yro_ref[i, 1].astype(F32)
        else:
            cacc_ref[i, :gp, :] += yri_ref[i, 0].astype(F32)
            cacc_ref[i, 2 * gp :, :] += yri_ref[i, 1].astype(F32)

    row_copies = {}

    def rows_out(b, i):
        columns_done(b, i)
        half = i // 2
        n = 2 * b + half
        cs_ref[n] = cacc_ref[3 * b + i].astype(BF16)
        row_copies[b, i] = send(
            cs_ref.at[n], cr_ref.at[n], ss_c.at[n], rs_c.at[n], along(hops[b] * (1 - i))
        )

    outer_taps(0)
    outer_taps(2)
    inner_taps(0)
    rows_out(1, 0)
    inner_taps(2)
    rows_out(1, 2)
    outer_taps(1)
    rows_out(0, 0)
    rows_out(0, 2)
    inner_taps(1)
    columns_done(0, 1)
    columns_done(1, 1)

    def inside(b, i):
        source = row + hops[b] * (i - 1)
        return jnp.logical_and(source >= 0, source < nrow)

    point_pre = []
    for b in (0, 1):
        total = cacc_ref[3 * b + 1]
        for i in (0, 2):
            row_copies[b, i].wait_recv()
            total = total + jnp.where(inside(b, i), cr_ref[2 * b + i // 2].astype(F32), 0.0)
        point_pre.append(total)

    sig = [jax.nn.sigmoid(v) for v in point_pre]
    joined = jnp.concatenate([(v * s).astype(BF16) for v, s in zip(point_pre, sig)], axis=1)
    proj_pre = dot(joined, proj_ref[...])
    proj_sig = jax.nn.sigmoid(proj_pre)
    projected = (proj_pre * proj_sig).astype(BF16)
    logits = dot(projected, cls_ref[...])
    lane = lax.broadcasted_iota(jnp.int32, logits.shape, 1)
    real = lane < 3
    top = jnp.max(jnp.where(real, logits, -jnp.inf), axis=1, keepdims=True)
    power = jnp.where(real, jnp.exp(jnp.where(real, logits - top, 0.0)), 0.0)
    soft = power / jnp.sum(power, axis=1, keepdims=True)
    onehot = (lane == lab_ref[...]).astype(F32)
    grad_logits = (LOSS_SCALE * (soft - onehot)).astype(BF16)
    grad_proj = (dot(grad_logits, cls_ref[...], NT) * slope(proj_pre, proj_sig)).astype(BF16)
    grad_joined = dot(grad_proj, proj_ref[...], NT)
    grad_act = [
        (grad_joined[:, b * outc : (b + 1) * outc] * slope(point_pre[b], sig[b])).astype(BF16)
        for b in (0, 1)
    ]
    g0_ref[1, 1:4] = grad_act[0].reshape(3, gp, outc)
    g1_ref[1, 3:6] = grad_act[1].reshape(3, gp, outc)

    z_copies = {}
    g_copies = {}
    refs = (g0_ref, g1_ref)

    def rows_back(b, i):
        own = slice(1, 4) if b == 0 else slice(3, 6)
        n = 2 * b + i // 2
        z_copies[b, i] = send(
            refs[b].at[1, own], refs[b].at[i, own], ss_gz.at[n], rs_gz.at[n],
            along(hops[b] * (i - 1)),
        )

    def columns_back(b, i):
        n = 2 * (3 * b + i)
        if b == 0:
            ends = ((slice(3, 4), slice(0, 1), right), (slice(1, 2), slice(4, 5), left))
        else:
            ends = ((slice(3, 6), slice(0, 3), right), (slice(3, 6), slice(6, 9), left))
        g_copies[b, i] = [
            send(refs[b].at[i, src], refs[b].at[i, dst], ss_gl.at[n + e], rs_gl.at[n + e], device)
            for e, (src, dst, device) in enumerate(ends)
        ]

    for b in (0, 1):
        for i in (0, 2):
            rows_back(b, i)
    columns_back(0, 1)
    columns_back(1, 1)
    for i in (0, 2):
        z_copies[0, i].wait_recv()
        columns_back(0, i)

    for b in (0, 1):
        for i in (0, 2):
            first = b * 9 + i * 3
            source = row - hops[b] * (i - 1)
            keep = jnp.logical_and(source >= 0, source < nrow).astype(F32)
            kf_ref[first : first + 3, :] = kf_ref[first : first + 3, :] * keep

    def window(b, i, j):
        start = 2 - j if b == 0 else 3 * (2 - j)
        return refs[b][i, start : start + 3].reshape(pix, outc)

    tile = 256
    tiles = channels // tile
    chunk = outc // ndp
    half_rows = chunk // 2

    def turned(b, i):
        for j in range(3):
            block = window(b, i, j).astype(F32)
            block = jnp.concatenate([block, jnp.zeros((pix_pad - pix, outc), F32)], axis=0)
            gt_ref[3 * i + j] = block.T.astype(BF16)

    def point_terms(b):
        def step(n, carry):
            cols = pl.ds(pl.multiple_of(n * tile, tile), tile)
            terms = dot(gt_ref[...].reshape(9 * outc, pix_pad), x_ref[:, cols])
            total = None
            for t in range(9):
                term = terms[t * outc : (t + 1) * outc] * kf_ref[b * 9 + t : b * 9 + t + 1, cols]
                total = term if total is None else total + term
            t_ref[b, :, :, :, cols] = total.astype(BF16).reshape(ndp, 2, half_rows, tile)
            return carry

        lax.fori_loop(0, tiles, step, 0)

    def input_terms(b):
        def step(n, carry):
            cols = pl.ds(pl.multiple_of(n * tile, tile), tile)
            weights = pw_ref[b, cols, :]
            total = None
            for i in range(3):
                if b == 0:
                    spread = dot(g0_ref[i].reshape(5 * gp, outc), weights, NT)
                else:
                    spread = dot(g1_ref[i].reshape(9 * gp, outc), weights, NT)
                for j in range(3):
                    start = (2 - j) * gp if b == 0 else (2 - j) * pix
                    t = b * 9 + 3 * i + j
                    term = spread[start : start + pix] * kf_ref[t : t + 1, cols]
                    total = term if total is None else total + term
            if b == 0:
                igacc_ref[:, cols] = total
            else:
                ig_ref[:, cols] = (igacc_ref[:, cols] + total).astype(BF16)
            return carry

        lax.fori_loop(0, tiles, step, 0)

    def core_out(b):
        return send(
            t_ref.at[b, :, 1 - core], rc_ref.at[b], ss_core.at[b], rs_core.at[b], partner
        )

    def core_in(b, copy):
        copy.wait_recv()
        s_ref[b] = (t_ref[b, :, core].astype(F32) + rc_ref[b].astype(F32)).astype(BF16)

    zc = channels // nz

    def z_cols(k):
        return pl.ds(pl.multiple_of(z_peer(k) * zc, zc), zc)

    def collect(copies, own, buffer):
        total = own.astype(F32)
        for k, copy in copies:
            copy.wait_recv()
            total = total + buffer[k].astype(F32)
        return total

    for i in range(3):
        for copy in g_copies[0, i]:
            copy.wait_recv()
        turned(0, i)
    point_terms(0)
    core0 = core_out(0)
    for i in (0, 2):
        z_copies[1, i].wait_recv()
        columns_back(1, i)
    input_terms(0)
    core_in(0, core0)
    y0_copies = [
        (k, send(s_ref.at[0, dp_peer(k)], ry_ref.at[k], ss_ry.at[k], rs_ry.at[k], {"dp": dp_peer(k)}))
        for k in range(1, ndp)
    ]

    for i in (1, 0, 2):
        for copy in g_copies[1, i]:
            copy.wait_recv()
        turned(1, i)
    point_terms(1)
    core1 = core_out(1)
    core_in(1, core1)
    z1_copies = [
        (k, send(
            s_ref.at[1, :, :, z_cols(k)], rz1_ref.at[k], ss_rz.at[k], rs_rz.at[k],
            {"row": z_peer(k) * 2 + xh},
        ))
        for k in range(1, nz)
    ]
    input_terms(1)

    u0_ref[...] = collect(y0_copies, s_ref[0, y], ry_ref).astype(BF16)
    z0_copies = [
        (k, send(
            u0_ref.at[:, z_cols(k)], rz0_ref.at[k], ss_rz.at[nz + k], rs_rz.at[nz + k],
            {"row": z_peer(k) * 2 + xh},
        ))
        for k in range(1, nz)
    ]
    u1_ref[...] = collect(z1_copies, s_ref[1, :, :, z_cols(0)], rz1_ref).astype(BF16)
    y1_copies = [
        (k, send(u1_ref.at[dp_peer(k)], ry1_ref.at[k], ss_ry.at[ndp + k], rs_ry.at[ndp + k], {"dp": dp_peer(k)}))
        for k in range(1, ndp)
    ]
    v_ref[0] = collect(z0_copies, u0_ref[:, z_cols(0)], rz0_ref)
    x_copies = [[], []]
    for b in (0, 1):
        if b == 1:
            v_ref[1] = collect(y1_copies, u1_ref[y], ry1_ref)
        x_copies[b] = [
            (k, send(
                v_ref.at[b], rx_ref.at[b, k], ss_rx.at[b * 2 * nlon + k], rs_rx.at[b * 2 * nlon + k], x_peer(k)
            ))
            for k in range(1, 2 * nlon)
        ]
    width = pg_ref.shape[1]
    pick = lax.broadcasted_iota(jnp.int32, (width, zc), 1) == (
        member * width + lax.broadcasted_iota(jnp.int32, (width, zc), 0)
    )
    pick = pick.astype(F32)
    for b in (0, 1):
        sums = [v_ref[b], None]
        for k, copy in x_copies[b]:
            copy.wait_recv()
            part = rx_ref[b, k]
            sums[k % 2] = part if sums[k % 2] is None else sums[k % 2] + part
        low = jnp.where(core == 0, sums[0], sums[1])
        high = jnp.where(core == 0, sums[1], sums[0])
        block = jnp.concatenate([low, high], axis=0)
        pg_ref[b] = scale * lax.dot_general(
            pick, block, NT, preferred_element_type=F32, precision=lax.Precision.HIGHEST
        )
    for copy in started:
        copy.wait_send()


def shards(features, depthwise_kernels, point_weights, proj_weight, class_weight, labels):
    rows, cols, channels = features.shape[1:]
    outc = point_weights.shape[2]
    classes = class_weight.shape[1]
    ndp, nrow, nlon = (lax.axis_size(a) for a in ("dp", "row", "lon"))
    nz = nrow // 2
    hops = (DILATION_INNER // rows, DILATION_OUTER // rows)
    groups = cols // GROUP
    real = rows * GROUP
    gp = -(-real // 16) * 16
    pix = groups * gp
    pix_pad = -(-pix // 128) * 128
    zc = channels // nz
    half = outc // ndp // 2
    chunk = channels // (nrow * nlon)
    scale = 1.0 / math.sqrt(ndp * nrow * nlon * rows * cols)

    x = features[0].reshape(rows, groups, GROUP, channels).transpose(1, 0, 2, 3)
    x = jnp.pad(x.reshape(groups, real, channels), ((0, 0), (0, gp - real), (0, 0)))
    x = jnp.pad(x.reshape(pix, channels), ((0, pix_pad - pix), (0, 0)))
    lab = labels[0].reshape(rows, groups, GROUP).transpose(1, 0, 2).reshape(groups, real)
    lab = jnp.pad(lab, ((0, 0), (0, gp - real))).reshape(pix, 1)
    cls = jnp.pad(class_weight, ((0, 0), (0, 128 - classes)))

    vmem = pl.BlockSpec(memory_space=pltpu.VMEM)
    dma = lambda n: pltpu.SemaphoreType.DMA((n,))
    scratch = [
        pltpu.VMEM((18, channels), F32),
        pltpu.VMEM((18, 16, channels), BF16),
        pltpu.VMEM((6, pix, outc), F32),
        pltpu.VMEM((3, 2, pix, outc), BF16),
        pltpu.VMEM((3, 2, pix, outc), BF16),
        pltpu.VMEM((3, 2, gp, outc), BF16),
        pltpu.VMEM((3, 2, gp, outc), BF16),
        pltpu.VMEM((4, pix, outc), BF16),
        pltpu.VMEM((4, pix, outc), BF16),
        pltpu.VMEM((3, 5, gp, outc), BF16),
        pltpu.VMEM((3, 9, gp, outc), BF16),
        pltpu.VMEM((9, outc, pix_pad), BF16),
        pltpu.VMEM((pix, channels), F32),
        pltpu.VMEM((2, ndp, 2, half, channels), BF16),
        pltpu.VMEM((2, ndp, half, channels), BF16),
        pltpu.VMEM((2, ndp, half, channels), BF16),
        pltpu.VMEM((ndp, half, channels), BF16),
        pltpu.VMEM((half, channels), BF16),
        pltpu.VMEM((nz, half, zc), BF16),
        pltpu.VMEM((nz, ndp, half, zc), BF16),
        pltpu.VMEM((ndp, half, zc), BF16),
        pltpu.VMEM((ndp, half, zc), BF16),
        pltpu.VMEM((2, half, zc), F32),
        pltpu.VMEM((2, 2 * nlon, half, zc), F32),
        dma(12), dma(12), dma(4), dma(4), dma(4), dma(4), dma(12), dma(12),
        dma(2), dma(2), dma(2 * ndp), dma(2 * ndp), dma(2 * nz), dma(2 * nz),
        dma(4 * nlon), dma(4 * nlon),
    ]
    input_grad, point_grad = pl.pallas_call(
        functools.partial(kernel, (ndp, nrow, nlon), hops, scale),
        out_shape=(
            jax.ShapeDtypeStruct((pix, channels), BF16),
            jax.ShapeDtypeStruct((2, chunk, outc // ndp), F32),
        ),
        in_specs=[vmem] * 6,
        out_specs=(vmem, vmem),
        scratch_shapes=scratch,
        compiler_params=pltpu.CompilerParams(
            collective_id=0, has_side_effects=True, vmem_limit_bytes=56 * 1024 * 1024
        ),
        cost_estimate=pl.CostEstimate(
            flops=54 * 2 * pix * channels * outc, bytes_accessed=8 * pix * channels, transcendentals=0
        ),
    )(x, depthwise_kernels.reshape(18, channels), point_weights, proj_weight, cls, lab)
    input_grad = input_grad.reshape(groups, gp, channels)[:, :real]
    input_grad = input_grad.reshape(groups, rows, GROUP, channels).transpose(1, 0, 2, 3)
    return input_grad.reshape(1, rows, cols, channels), point_grad


def solution(mesh):
    placed = (P("dp", "row", "lon", None), P(), P(), P(), P(), P("dp", "row", "lon"))
    return jax.shard_map(
        shards,
        mesh=mesh,
        in_specs=placed,
        out_specs=(P("dp", "row", "lon", None), P(None, ("row", "lon"), "dp")),
        check_vma=False,
    )
```

time: 394 us -> 99.9 us (0.25); the launches traced: 388 us -> 99.3 us
  waiting for transfers between devices: 241 us -> 0 us
  starting transfers between devices: 92.3 us -> 0 us
  Pallas kernels: 0 us -> 90.1 us
  other arithmetic: 25.7 us -> 0.01 us
  between operations: 14.3 us -> 0.73 us
  matrix products: 8.44 us -> 0 us
    reduce_scatter x1 -> x0, waiting for transfers between devices: 129 us -> none  [shards(): lax.psum_scatter(jnp.stack(point_terms), ('row', 'lon'), scatter_dimensio...]
    ppermute x14 -> x0, starting transfers between devices: 92.2 us -> none  [the longest x8 69.9 us: passed_along(): return lax.ppermute(block, axis, route)]
    pallas_call x0 -> x1, Pallas kernels: none -> 90.1 us  [shards(): pl.pallas_call(functools.partial(kernel, (ndp, nrow, nlon), hops, scale),...]
    ppermute x14 -> x0, waiting for transfers between devices: 79.7 us -> none  [the longest x8 43.7 us: passed_along(): return lax.ppermute(block, axis, route)]
    unnamed x3 -> x0, waiting for transfers between devices: 32.6 us -> none
    convert_element_type x10 -> x0, other arithmetic: 22.8 us -> none  [the longest x4 12 us: row_partials(): partials.append(total_sum.astype(jnp.bfloat16))]
    dot_general x9 -> x0, matrix products: 8.44 us -> none  [the longest x2 4.36 us: shards(): jnp.dot(grad_act, point_weights[branch_index].T, preferred_element_type=j...]
  transfers between devices with their start and end apart: 16 -> 0, of which waited for: 10 -> 0; matrix products, arithmetic and copies ran while one was open for 5% -> 0% of each run, Pallas kernels for 0% -> 0%
where the time goes in v1:
time: 99.9 us; the launch traced here: 99.3 us
  Pallas kernels  90.1 us (90%)
  local copies, waits for them, and re-layouts  8.54 us (9%)
    pallas_call x1, Pallas kernels, shards(): pl.pallas_call(functools.partial(kernel, (ndp, nrow, nlon), hops, scale),...  90.1 us

profile of v1, /device:TPU:1, one launch (start us, length us, event | category | flops | bytes accessed | tf_op | source)
XLA Modules:
  0.0 99.3 jit_solution(17048310399663204208)
XLA Ops:
  0.6 1.3 %reshape_squeeze.6 = bf16[6,3,12,2048]{3,2,1,0:T(8,128)(2,1)S(1)} reshape(bf16[1,6,36,2048]{3,2,1,0:T(8,128)(2,1)} %param.6) | data formatting | bytes 1769472 | tf_op jit(solution)/shard_map/reshape;squeeze | solution.py:404
  1.9 0.1 copy.13
  2.0 0.2 reshape.28
  2.2 0.1 pad.16
  2.4 0.0 copy-start
  2.4 0.0 copy-start.2
  2.4 0.0 copy-start.3
  2.4 1.1 %pad.17.x_ref = bf16[256,2048]{1,0:T(8,128)(2,1)} pad(bf16[240,2048]{1,0:T(8,128)(2,1)S(1)} %bitcast.9, bf16[]{:T(256)} %constant.2.clone.1), padding=0_16x0_0 | pad | bytes 2031618 | tf_op jit(solution)/shard_map/jit(_pad)/pad | solution.py:406
  3.5 0.0 copy-done
  3.5 0.1 copy.14
  3.5 0.7 reshape.30.k_ref
  4.2 0.0 copy-done.2
  4.3 0.1 reshape_squeeze.7
  4.4 0.1 reshape.31
  4.4 0.8 reshape.36.lab_ref
  5.3 0.0 copy-done.3
  5.3 0.1 copy.15
  5.4 0.6 pad.18.cls_ref
  6.0 90.1 %shard_map.77 = (bf16[240,2048]{1,0:T(8,128)(2,1)}, f32[2,32,32]{2,1,0:T(8,128)}) custom-call(bf16[256,2048]{1,0:T(8,128)(2,1)} %pad.17.x_ref, bf16[18,2048]{1,0:T(8,128)(2,1)} %reshape.30.k_ref, bf16[2,2048,256]{2,1,0:T(8,128)(2,1)} %pw_ref.1, bf16[512,256]{1,0:T(8,128)(2,1)} %proj_ref.1, bf16[256,128]{1,0:T(8,128)(2,1)} %pad.18.cls_ref, ...), custom_call_target="tpu_custom_call" | custom-call | flops 13589544960 | bytes 3932160 | tf_op jit(solution)/shard_map/pallas_call | solution.py:442
  96.1 1.2 %slice.4 = bf16[3,72,2048]{2,1,0:T(8,128)(2,1)S(1)} slice(bf16[3,80,2048]{2,1,0:T(8,128)(2,1)} %bitcast.10), slice={[0:3], [0:72], [0:2048]} | slice | bytes 1769472 | tf_op jit(solution)/shard_map/slice | solution.py:458
  97.3 0.2 reshape.34
  97.5 0.1 copy.20
  97.7 0.0 copy-start.1
  97.7 1.0 %reshape.35 = bf16[1,6,36,2048]{3,2,1,0:T(8,128)(2,1)} reshape(bf16[6,3,12,2048]{3,2,1,0:T(8,128)(2,1)S(1)} %bitcast.7) | data formatting | bytes 1769472 | tf_op jit(solution)/shard_map/reshape | solution.py:460
  98.7 0.0 copy-done.1
  98.7 0.6 copy.22
  (3 shorter events, 0.0 us)
Async XLA Ops:
  2.4 1.1 %copy-start = (bf16[2,3,3,2048]{3,0,2,1:T(2,128)(2,1)S(1)}, bf16[2,3,3,2048]{3,0,2,1:T(2,128)(2,1)}, u32[]{:S(2)}) copy-start(bf16[2,3,3,2048]{3,0,2,1:T(2,128)(2,1)} %param.7) | copy-start | bytes 221188
  2.4 1.9 %copy-start.2 = (s32[1,6,36]{2,0,1:T(1,128)S(1)}, s32[1,6,36]{2,0,1:T(1,128)}, u32[]{:S(2)}) copy-start(s32[1,6,36]{2,0,1:T(1,128)} %param.11) | copy-start | bytes 2596
  2.4 2.9 %copy-start.3 = (bf16[256,3]{0,1:T(4,128)(2,1)S(1)}, bf16[256,3]{0,1:T(4,128)(2,1)}, u32[]{:S(2)}) copy-start(bf16[256,3]{0,1:T(4,128)(2,1)} %param.10) | copy-start | bytes 4612
  97.7 1.1 %copy-start.1 = (f32[2,32,32]{2,1,0:T(8,128)S(1)}, f32[2,32,32]{2,1,0:T(8,128)}, u32[]{:S(2)}) copy-start(f32[2,32,32]{2,1,0:T(8,128)} %get-tuple-element.9) | copy-start | bytes 24580

commit v2 on v1

v2 whole, which is shorter than its diff:
```python
import functools
import math

import jax
import jax.numpy as jnp
from jax import lax
from jax.experimental import pallas as pl
from jax.experimental.pallas import tpu as pltpu
from jax.sharding import PartitionSpec as P

DILATION_INNER = 12
DILATION_OUTER = 36
GROUP = DILATION_INNER
LOSS_SCALE = 32.0
MESH = pl.DeviceIdType.MESH
NN = (((1,), (0,)), ((), ()))
NT = (((1,), (1,)), ((), ()))
F32 = jnp.float32
BF16 = jnp.bfloat16


def dot(a, b, dims=NN):
    return lax.dot_general(a, b, dims, preferred_element_type=F32)


def slope(value, sigma):
    return sigma * (1.0 + value * (1.0 - sigma))


def pixel_places(axis, shape, gp, rows, pitch):
    m = lax.broadcasted_iota(jnp.int32, shape, axis)
    zero = jnp.zeros(shape, jnp.int32)
    group = zero
    for g in (1, 2):
        group = group + jnp.where(m >= g * gp, 1, 0)
    rest = m - group * gp
    row = zero
    for r in range(1, rows):
        row = row + jnp.where(rest >= r * GROUP, 1, 0)
    col = rest - row * GROUP
    real = jnp.logical_and(rest < rows * GROUP, m < 3 * gp)
    return row, group * GROUP + col, jnp.where(real, row * pitch + group * GROUP + col, -1)


def kernel(
    size, hops, scale,
    x_hbm, k_hbm, pw_hbm, proj_hbm, cls_hbm, lab_hbm,
    ig_hbm, pg_ref,
    x_ref, k_ref, pw_ref, proj_ref, cls_ref, lab_ref, ig_ref, in_sem, out_sem,
    xs_ref, xg_ref, put_ref, ls_ref, hot_ref, clsp_ref, kf_ref, kb_ref, cacc_ref,
    yso_ref, yro_ref, ysi_ref, yri_ref,
    cs_ref, cr_ref,
    g0_ref, g1_ref, gt_ref, igacc_ref, tacc_ref,
    t_ref, rc_ref, sa_ref, sb_ref, rya_ref, rzb_ref, ua_ref, ub_ref, rza_ref, ryb_ref, v_ref, rx_ref,
    ss_y, rs_y, ss_c, rs_c, ss_gz, rs_gz, ss_gl, rs_gl,
    ss_core, rs_core, ss_ya, rs_ya, ss_zb, rs_zb, ss_za, rs_za, ss_yb, rs_yb, ss_rx, rs_rx,
):
    ndp, nrow, nlon = size
    nz = nrow // 2
    rows, cols_dev, channels = x_ref.shape
    outc = pw_ref.shape[2]
    gp = g0_ref.shape[2]
    pix = 3 * gp
    pix_pad = xg_ref.shape[0]
    pitch = xs_ref.shape[1]
    y = lax.axis_index("dp")
    row = lax.axis_index("row")
    lon = lax.axis_index("lon")
    z = row // 2
    xh = row % 2
    core = lon % 2
    member = xh * nlon + lon
    right = {"lon": (lon + 1) % nlon}
    left = {"lon": (lon + nlon - 1) % nlon}
    partner = {"lon": lon + 1 - 2 * core}

    def along(shift):
        return {"row": (row + shift + nrow) % nrow}

    def dp_peer(k):
        return (y + k) % ndp

    def z_peer(k):
        return (z + k) % nz

    def z_device(k):
        return {"row": z_peer(k) * 2 + xh}

    def x_peer(k):
        other = (member + k) % (2 * nlon)
        return {"row": z * 2 + other // nlon, "lon": other % nlon}

    started = []

    def remote(src, dst, ssem, rsem, device):
        return pltpu.make_async_remote_copy(
            src_ref=src, dst_ref=dst, send_sem=ssem, recv_sem=rsem,
            device_id=device, device_id_type=MESH,
        )

    def send(*args):
        copy = remote(*args)
        copy.start()
        started.append(copy)
        return copy

    loads = [
        pltpu.make_async_copy(src, dst, in_sem.at[n])
        for n, (src, dst) in enumerate((
            (k_hbm, k_ref), (x_hbm.at[0], x_ref), (pw_hbm, pw_ref),
            (proj_hbm, proj_ref), (cls_hbm, cls_ref), (lab_hbm, lab_ref),
        ))
    ]
    for load in loads:
        load.start()

    barrier = pltpu.get_barrier_semaphore()
    peers = [left, right]
    for shift in hops:
        peers += [along(shift), along(-shift)]
    peers += [{"dp": dp_peer(k)} for k in range(1, ndp)]
    peers += [z_device(k) for k in range(1, nz)]
    peers += [x_peer(k) for k in range(1, 2 * nlon)]
    for peer in peers:
        pl.semaphore_signal(barrier, inc=1, device_id=peer, device_id_type=MESH)

    loads[0].wait()
    for i in range(3):
        for j in range(3):
            taps_ij = k_ref[i, j].astype(F32)
            for b in (0, 1):
                t = b * 9 + i * 3 + j
                kf_ref[t : t + 1, :] = taps_ij[b : b + 1]
    for t in range(18):
        kb_ref[t] = jnp.broadcast_to(kf_ref[t : t + 1, :], (16, channels)).astype(BF16)

    loads[1].wait()
    for r in range(rows):
        xs_ref[r, pitch - 16 :, :] = jnp.zeros((16, channels), BF16)
        xs_ref[r, :cols_dev, :] = x_ref[r]
    _, _, place = pixel_places(0, (pix_pad, rows * pitch), gp, rows, pitch)
    spot = lax.broadcasted_iota(jnp.int32, place.shape, 1)
    gather = (place == spot).astype(F32).astype(BF16)
    xg_ref[...] = dot(gather, xs_ref[...].reshape(rows * pitch, channels)).astype(BF16)
    loads[2].wait()

    def tap(b, i, j):
        x = xg_ref[:pix, :].reshape(pix // 16, 16, channels)
        scaled = (x * kb_ref[b * 9 + i * 3 + j][None]).reshape(pix, channels)
        return dot(scaled, pw_ref[b])

    group_rows = [slice(g * gp, (g + 1) * gp) for g in range(3)]
    lon_copies = {}

    def outer_send(i, g):
        n = 6 + (3 * i + g) * 2
        here = group_rows[g]
        lon_copies[1, i, g] = [
            send(yso_ref.at[i, e, here], yro_ref.at[i, e, here], ss_y.at[n + e], rs_y.at[n + e], device)
            for e, device in ((0, right), (1, left))
        ]

    def outer_sides(i):
        yso_ref[i, 0] = tap(1, i, 0).astype(BF16)
        yso_ref[i, 1] = tap(1, i, 2).astype(BF16)

    def inner_taps(i):
        y0 = tap(0, i, 0)
        ysi_ref[i, 0] = y0[2 * gp :].astype(BF16)
        y2 = tap(0, i, 2)
        ysi_ref[i, 1] = y2[:gp].astype(BF16)
        lon_copies[0, i] = [
            send(ysi_ref.at[i, e], yri_ref.at[i, e], ss_y.at[2 * i + e], rs_y.at[2 * i + e], device)
            for e, device in ((0, right), (1, left))
        ]
        cacc_ref[i] = tap(0, i, 1)
        cacc_ref[i, gp:, :] += y0[: 2 * gp]
        cacc_ref[i, : 2 * gp, :] += y2[gp:]

    def outer_done(i, g):
        for copy in lon_copies[1, i, g]:
            copy.wait_recv()
        here = group_rows[g]
        return cacc_ref[3 + i, here] + yro_ref[i, 0, here].astype(F32) + yro_ref[i, 1, here].astype(F32)

    def inner_done(i, g):
        total = cacc_ref[i, group_rows[g]]
        if g == 0:
            lon_copies[0, i][0].wait_recv()
            total = total + yri_ref[i, 0].astype(F32)
        if g == 2:
            lon_copies[0, i][1].wait_recv()
            total = total + yri_ref[i, 1].astype(F32)
        return total

    row_copies = {}

    def rows_out(b, i, g):
        here = group_rows[g]
        m = 2 * b + i // 2
        cs_ref[m, here] = (inner_done, outer_done)[b](i, g).astype(BF16)
        row_copies[b, i, g] = send(
            cs_ref.at[m, here], cr_ref.at[m, here], ss_c.at[3 * m + g], rs_c.at[3 * m + g],
            along(hops[b] * (1 - i)),
        )

    outer_sides(0)
    outer_sides(2)
    pl.semaphore_wait(barrier, len(peers))
    outer_send(0, 0)
    outer_send(2, 0)
    inner_taps(0)
    inner_taps(2)
    for g in (1, 2):
        outer_send(0, g)
        outer_send(2, g)
    cacc_ref[3] = tap(1, 0, 1)
    cacc_ref[5] = tap(1, 2, 1)
    outer_sides(1)
    outer_send(1, 0)
    inner_taps(1)
    for g in (1, 2):
        outer_send(1, g)
    for g in range(3):
        for b in (1, 0):
            for i in (0, 2):
                rows_out(b, i, g)
        if g == 0:
            cacc_ref[4] = tap(1, 1, 1)

    for load in loads[3:]:
        load.wait()
    ls_ref[...] = jnp.zeros_like(ls_ref)
    for r in range(rows):
        ls_ref[r : r + 1, :cols_dev] = lab_ref[r].astype(F32)
    wide = (pix, 128)
    lane = lax.broadcasted_iota(jnp.int32, wide, 1)
    pixel_row, pixel_col, _ = pixel_places(0, wide, gp, rows, pitch)
    by_row = dot((lane == pixel_row).astype(F32).astype(BF16), ls_ref[...].astype(BF16))
    label = jnp.sum(jnp.where(lane == pixel_col, by_row, 0.0), axis=1, keepdims=True)
    hot_ref[...] = (lane.astype(F32) == label).astype(F32)
    clsp_ref[...] = jnp.zeros_like(clsp_ref)
    clsp_ref[: cls_ref.shape[0], :] = cls_ref[...]
    _, _, place = pixel_places(1, (rows * pitch, pix_pad), gp, rows, pitch)
    spot = lax.broadcasted_iota(jnp.int32, place.shape, 0)
    put_ref[...] = (place == spot).astype(F32).astype(BF16)

    def inside(source):
        return jnp.logical_and(source >= 0, source < nrow)

    def head(g):
        here = group_rows[g]
        point_pre = []
        for b in (0, 1):
            total = (inner_done, outer_done)[b](1, g)
            for i in (0, 2):
                row_copies[b, i, g].wait_recv()
                term = cr_ref[2 * b + i // 2, here].astype(F32)
                total = total + jnp.where(inside(row + hops[b] * (i - 1)), term, 0.0)
            point_pre.append(total)
        sig = [jax.nn.sigmoid(v) for v in point_pre]
        joined = jnp.concatenate([(v * s).astype(BF16) for v, s in zip(point_pre, sig)], axis=1)
        proj_pre = dot(joined, proj_ref[...])
        proj_sig = jax.nn.sigmoid(proj_pre)
        projected = (proj_pre * proj_sig).astype(BF16)
        logits = dot(projected, clsp_ref[...], NT)
        real = lax.broadcasted_iota(jnp.int32, logits.shape, 1) < cls_ref.shape[0]
        top = jnp.max(jnp.where(real, logits, -jnp.inf), axis=1, keepdims=True)
        power = jnp.where(real, jnp.exp(jnp.where(real, logits - top, 0.0)), 0.0)
        soft = power / jnp.sum(power, axis=1, keepdims=True)
        grad_logits = (LOSS_SCALE * (soft - hot_ref[here])).astype(BF16)
        grad_proj = (dot(grad_logits, clsp_ref[...]) * slope(proj_pre, proj_sig)).astype(BF16)
        grad_joined = dot(grad_proj, proj_ref[...], NT)
        return [
            (grad_joined[:, b * outc : (b + 1) * outc] * slope(point_pre[b], sig[b])).astype(BF16)
            for b in (0, 1)
        ]

    z_copies = {}
    g_copies = {}

    def rows_back(b, i, g):
        ref = (g0_ref, g1_ref)[b]
        own = slice(1 + 2 * b + g, 2 + 2 * b + g)
        n = 3 * (2 * b + i // 2) + g
        z_copies[b, i, g] = send(
            ref.at[1, own], ref.at[i, own], ss_gz.at[n], rs_gz.at[n], along(hops[b] * (i - 1))
        )

    def inner_side(i, g):
        if g == 1:
            return
        src, dst, e, device = (
            (slice(3, 4), slice(0, 1), 0, right) if g == 2 else (slice(1, 2), slice(4, 5), 1, left)
        )
        g_copies[0, i, g] = [
            send(g0_ref.at[i, src], g0_ref.at[i, dst], ss_gl.at[2 * i + e], rs_gl.at[2 * i + e], device)
        ]

    def outer_side(i, g):
        n = 6 + 2 * (3 * i + g)
        src = slice(3 + g, 4 + g)
        g_copies[1, i, g] = [
            send(g1_ref.at[i, src], g1_ref.at[i, dst], ss_gl.at[n + e], rs_gl.at[n + e], device)
            for e, (dst, device) in enumerate(((slice(g, g + 1), right), (slice(6 + g, 7 + g), left)))
        ]

    for g in range(3):
        grads = head(g)
        g0_ref[1, 1 + g] = grads[0]
        g1_ref[1, 3 + g] = grads[1]
        for b in (0, 1):
            for i in (0, 2):
                rows_back(b, i, g)
        inner_side(1, g)
        outer_side(1, g)

    def pass_on(b, g):
        for i in (0, 2):
            z_copies[b, i, g].wait_recv()
            (inner_side, outer_side)[b](i, g)

    for b in (0, 1):
        for i in (0, 2):
            first = b * 9 + i * 3
            keep = inside(row - hops[b] * (i - 1)).astype(F32)
            kf_ref[first : first + 3, :] = kf_ref[first : first + 3, :] * keep

    zc = channels // nz
    hc = zc // 2
    half_rows = outc // ndp // 2

    def turned(b, i, j, slot):
        start = 2 - j if b == 0 else 3 * (2 - j)
        block = (g0_ref, g1_ref)[b][i, start : start + 3].reshape(pix, outc).astype(F32)
        block = jnp.concatenate([block, jnp.zeros((pix_pad - pix, outc), F32)], axis=0)
        gt_ref[slot] = block.T.astype(BF16)

    def z_cols(k):
        return pl.ds(pl.multiple_of(z_peer(k) * zc, zc), zc)

    def core_copy(b, k):
        n = z_peer(k)
        return remote(
            t_ref.at[b, n, 1 - core], rc_ref.at[b, n],
            ss_core.at[b * nz + k], rs_core.at[b * nz + k], partner,
        )

    def zb_copy(b, k):
        return remote(
            sb_ref.at[b, z_peer(k)], rzb_ref.at[b, k],
            ss_zb.at[b * nz + k], rs_zb.at[b * nz + k], z_device(k),
        )

    def point_terms(b, taps, first, last, steps=(0, None)):
        def step(s, carry):
            k = (s + 1) % nz
            cols = z_cols(k)
            terms = dot(gt_ref[: len(taps)].reshape(len(taps) * outc, pix_pad), xg_ref[:, cols])
            total = None if first else tacc_ref[:, cols]
            for slot, (i, j) in enumerate(taps):
                t = b * 9 + i * 3 + j
                term = terms[slot * outc : (slot + 1) * outc] * kf_ref[t : t + 1, cols]
                total = term if total is None else total + term
            if not last:
                tacc_ref[:, cols] = total
            else:
                block = total.astype(BF16).reshape(ndp, 2, half_rows, zc)
                for c in (0, 1):
                    t_ref[b, z_peer(k), c] = block[:, c]
                core_copy(b, k).start()
            return carry

        lax.fori_loop(steps[0], nz if steps[1] is None else steps[1], step, 0)

    def chip_sums(b):
        def add(k):
            core_copy(b, k).wait_recv()
            n = z_peer(k)
            total = (t_ref[b, n, core].astype(F32) + rc_ref[b, n].astype(F32)).astype(BF16)
            sb_ref[b, n] = total[:, :, hc:]
            sa_ref[b, :, n] = total[:, :, :hc]

        def step(s, carry):
            add(s + 1)
            zb_copy(b, s + 1).start()
            return carry

        lax.fori_loop(0, nz - 1, step, 0)
        add(0)
        return [
            (k, send(
                sa_ref.at[b, dp_peer(k)], rya_ref.at[b, k],
                ss_ya.at[b * ndp + k], rs_ya.at[b * ndp + k], {"dp": dp_peer(k)},
            ))
            for k in range(1, ndp)
        ]

    def collect(copies, own, buffer):
        total = own.astype(F32)
        for k, copy in copies:
            copy.wait_recv()
            total = total + buffer[k].astype(F32)
        return total

    def second(b, ya):
        ua_ref[b] = collect(ya, sa_ref[b, y], rya_ref.at[b]).astype(BF16)
        za = [
            (k, send(
                ua_ref.at[b, z_peer(k)], rza_ref.at[b, k],
                ss_za.at[b * nz + k], rs_za.at[b * nz + k], z_device(k),
            ))
            for k in range(1, nz)
        ]
        zb = [(k, zb_copy(b, k)) for k in range(1, nz)]
        ub_ref[b] = collect(zb, sb_ref[b, z], rzb_ref.at[b]).astype(BF16)
        yb = [
            (k, send(
                ub_ref.at[b, dp_peer(k)], ryb_ref.at[b, k],
                ss_yb.at[b * ndp + k], rs_yb.at[b * ndp + k], {"dp": dp_peer(k)},
            ))
            for k in range(1, ndp)
        ]
        return za, yb

    def third(b, za, yb):
        part_a = collect(za, ua_ref[b, z], rza_ref.at[b])
        part_b = collect(yb, ub_ref[b, y], ryb_ref.at[b])
        v_ref[b] = jnp.concatenate([part_a, part_b], axis=1).astype(BF16)
        return [
            (k, send(
                v_ref.at[b], rx_ref.at[b, k],
                ss_rx.at[b * 2 * nlon + k], rs_rx.at[b * 2 * nlon + k], x_peer(k),
            ))
            for k in range(1, 2 * nlon)
        ]

    def input_terms(b):
        def step(n, carry):
            cols = pl.ds(pl.multiple_of(n * zc, zc), zc)
            weights = pw_ref[b, cols, :]
            total = None
            for i in range(3):
                if b == 0:
                    spread = dot(g0_ref[i].reshape(5 * gp, outc), weights, NT)
                else:
                    spread = dot(g1_ref[i].reshape(9 * gp, outc), weights, NT)
                for j in range(3):
                    start = (2 - j) * gp if b == 0 else (2 - j) * pix
                    t = b * 9 + 3 * i + j
                    term = spread[start : start + pix] * kf_ref[t : t + 1, cols]
                    total = term if total is None else total + term
            if b == 0:
                igacc_ref[:, cols] = total
            else:
                total = (igacc_ref[:, cols] + total).astype(BF16)
                total = jnp.concatenate([total, jnp.zeros((pix_pad - pix, zc), BF16)], axis=0)
                placed = dot(put_ref[...], total).astype(BF16)
                for r in range(rows):
                    ig_ref[r, :, cols] = placed[r * pitch : r * pitch + cols_dev]
            return carry

        lax.fori_loop(0, nz, step, 0)

    pass_on(0, 0)
    pass_on(1, 0)
    for g in range(3):
        for copy in g_copies[1, 1, g]:
            copy.wait_recv()
    for j in range(3):
        turned(1, 1, j, j)
    point_terms(1, [(1, j) for j in range(3)], True, False)
    pass_on(0, 1)
    pass_on(1, 1)
    pass_on(0, 2)
    for i in range(3):
        for g in (0, 2):
            for copy in g_copies[0, i, g]:
                copy.wait_recv()
        for j in range(3):
            turned(0, i, j, 3 * i + j)
    inner = [(i, j) for i in range(3) for j in range(3)]
    point_terms(0, inner, True, True, (0, nz // 2))
    pass_on(1, 2)
    point_terms(0, inner, True, True, (nz // 2, nz))
    ya0 = chip_sums(0)
    middle = [(0, 1), (2, 1)]
    for slot, (i, j) in enumerate(middle):
        turned(1, i, j, slot)
    point_terms(1, middle, False, False)
    sides = [(i, j) for i in (0, 2) for j in (0, 2)]
    for i in (0, 2):
        for g in range(3):
            for copy in g_copies[1, i, g]:
                copy.wait_recv()
    for slot, (i, j) in enumerate(sides):
        turned(1, i, j, slot)
    point_terms(1, sides, False, True)
    ya1 = chip_sums(1)
    input_terms(0)
    za0, yb0 = second(0, ya0)
    input_terms(1)
    ig_out = pltpu.make_async_copy(ig_ref, ig_hbm.at[0], out_sem)
    ig_out.start()

    za1, yb1 = second(1, ya1)
    x_copies = [third(0, za0, yb0)]
    x_copies.append(third(1, za1, yb1))
    width = pg_ref.shape[1]
    pick = lax.broadcasted_iota(jnp.int32, (width, zc), 1) == (
        member * width + lax.broadcasted_iota(jnp.int32, (width, zc), 0)
    )
    pick = pick.astype(F32)
    for b in (0, 1):
        sums = [v_ref[b].astype(F32), None]
        for k, copy in x_copies[b]:
            copy.wait_recv()
            part = rx_ref[b, k].astype(F32)
            sums[k % 2] = part if sums[k % 2] is None else sums[k % 2] + part
        low = jnp.where(core == 0, sums[0], sums[1])
        high = jnp.where(core == 0, sums[1], sums[0])
        block = jnp.concatenate([low, high], axis=0)
        pg_ref[b] = scale * lax.dot_general(
            pick, block, NT, preferred_element_type=F32, precision=lax.Precision.HIGHEST
        )
    ig_out.wait()
    for copy in started:
        copy.wait_send()

    def finish(k, carry):
        for b in (0, 1):
            core_copy(b, k).wait_send()
        return carry

    lax.fori_loop(0, nz, finish, 0)

    def finish_z(k, carry):
        for b in (0, 1):
            zb_copy(b, k).wait_send()
        return carry

    lax.fori_loop(1, nz, finish_z, 0)


def shards(features, depthwise_kernels, point_weights, proj_weight, class_weight, labels):
    rows, cols, channels = features.shape[1:]
    outc = point_weights.shape[2]
    ndp, nrow, nlon = (lax.axis_size(a) for a in ("dp", "row", "lon"))
    nz = nrow // 2
    hops = (DILATION_INNER // rows, DILATION_OUTER // rows)
    groups = cols // GROUP
    gp = -(-rows * GROUP // 16) * 16
    pix = groups * gp
    pix_pad = -(-pix // 128) * 128
    pitch = -(-cols // 16) * 16
    zc = channels // nz
    hc = zc // 2
    half = outc // ndp // 2
    chunk = channels // (nrow * nlon)
    scale = 1.0 / math.sqrt(ndp * nrow * nlon * rows * cols)

    vmem = pl.BlockSpec(memory_space=pltpu.VMEM)
    hbm = pl.BlockSpec(memory_space=pl.ANY)
    kernels = depthwise_kernels.transpose(1, 2, 0, 3)
    classes = class_weight.T
    label_rows = labels.transpose(1, 0, 2)
    dma = lambda n: pltpu.SemaphoreType.DMA((n,))
    scratch = [
        pltpu.VMEM(features.shape[1:], BF16),
        pltpu.VMEM(kernels.shape, BF16),
        pltpu.VMEM(point_weights.shape, BF16),
        pltpu.VMEM(proj_weight.shape, BF16),
        pltpu.VMEM(classes.shape, BF16),
        pltpu.VMEM(label_rows.shape, jnp.int32),
        pltpu.VMEM(features.shape[1:], BF16),
        dma(6), pltpu.SemaphoreType.DMA,
        pltpu.VMEM((rows, pitch, channels), BF16),
        pltpu.VMEM((pix_pad, channels), BF16),
        pltpu.VMEM((rows * pitch, pix_pad), BF16),
        pltpu.VMEM((128, 128), F32),
        pltpu.VMEM((pix, 128), F32),
        pltpu.VMEM((128, outc), BF16),
        pltpu.VMEM((18, channels), F32),
        pltpu.VMEM((18, 16, channels), BF16),
        pltpu.VMEM((6, pix, outc), F32),
        pltpu.VMEM((3, 2, pix, outc), BF16),
        pltpu.VMEM((3, 2, pix, outc), BF16),
        pltpu.VMEM((3, 2, gp, outc), BF16),
        pltpu.VMEM((3, 2, gp, outc), BF16),
        pltpu.VMEM((4, pix, outc), BF16),
        pltpu.VMEM((4, pix, outc), BF16),
        pltpu.VMEM((3, 5, gp, outc), BF16),
        pltpu.VMEM((3, 9, gp, outc), BF16),
        pltpu.VMEM((9, outc, pix_pad), BF16),
        pltpu.VMEM((pix, channels), F32),
        pltpu.VMEM((outc, channels), F32),
        pltpu.VMEM((2, nz, 2, ndp, half, zc), BF16),
        pltpu.VMEM((2, nz, ndp, half, zc), BF16),
        pltpu.VMEM((2, ndp, nz, half, hc), BF16),
        pltpu.VMEM((2, nz, ndp, half, hc), BF16),
        pltpu.VMEM((2, ndp, nz, half, hc), BF16),
        pltpu.VMEM((2, nz, ndp, half, hc), BF16),
        pltpu.VMEM((2, nz, half, hc), BF16),
        pltpu.VMEM((2, ndp, half, hc), BF16),
        pltpu.VMEM((2, nz, half, hc), BF16),
        pltpu.VMEM((2, ndp, half, hc), BF16),
        pltpu.VMEM((2, half, zc), BF16),
        pltpu.VMEM((2, 2 * nlon, half, zc), BF16),
        dma(24), dma(24), dma(12), dma(12), dma(12), dma(12), dma(24), dma(24),
        dma(2 * nz), dma(2 * nz), dma(2 * ndp), dma(2 * ndp), dma(2 * nz), dma(2 * nz),
        dma(2 * nz), dma(2 * nz), dma(2 * ndp), dma(2 * ndp), dma(4 * nlon), dma(4 * nlon),
    ]
    return pl.pallas_call(
        functools.partial(kernel, (ndp, nrow, nlon), hops, scale),
        out_shape=(
            jax.ShapeDtypeStruct(features.shape, BF16),
            jax.ShapeDtypeStruct((2, chunk, outc // ndp), F32),
        ),
        in_specs=[hbm] * 6,
        out_specs=(hbm, vmem),
        scratch_shapes=scratch,
        compiler_params=pltpu.CompilerParams(
            collective_id=0, has_side_effects=True, vmem_limit_bytes=56 * 1024 * 1024
        ),
        cost_estimate=pl.CostEstimate(
            flops=54 * 2 * pix * channels * outc, bytes_accessed=8 * pix * channels, transcendentals=0
        ),
    )(features, kernels, point_weights, proj_weight, classes, label_rows)


def solution(mesh):
    placed = (P("dp", "row", "lon", None), P(), P(), P(), P(), P("dp", "row", "lon"))
    return jax.shard_map(
        shards,
        mesh=mesh,
        in_specs=placed,
        out_specs=(P("dp", "row", "lon", None), P(None, ("row", "lon"), "dp")),
        check_vma=False,
    )
```

time: 99.9 us -> 84.5 us (0.85)
  Pallas kernels: 90.1 us -> 80 us
  local copies, waits for them, and re-layouts: 8.54 us -> 3.62 us
    pallas_call x1, Pallas kernels: 90.1 us -> 80 us  [shards(): pl.pallas_call(functools.partial(kernel, (ndp, nrow, nlon), hops, scale),...]
    reshape x7 -> x0, local copies, waits for them, and re-layouts: 3.16 us -> none  [the longest x1 1.04 us: shards(): return (input_grad.reshape(1, rows, cols, channels), point_grad)]
    unnamed x11 -> x2, local copies, waits for them, and re-layouts: 0.84 us -> 3.62 us
    pad x4 -> x0, local copies, waits for them, and re-layouts: 1.83 us -> none  [the longest x1 1.07 us: shards(): x = jnp.pad(x.reshape(pix, channels), ((0, pix_pad - pix), (0, 0)))]
    another operation x2 -> x0, local copies, waits for them, and re-layouts: 1.36 us -> none  [the longest x1 1.28 us: shards(): x = features[0].reshape(rows, groups, GROUP, channels).transpose(1, 0, 2, 3)]
    slice x1 -> x0, local copies, waits for them, and re-layouts: 1.23 us -> none  [shards(): input_grad = input_grad.reshape(groups, gp, channels)[:, :real]]
where the time goes in v2:
time: 84.5 us; the launch traced here: 84.3 us
  Pallas kernels  80 us (95%)
  local copies, waits for them, and re-layouts  3.62 us (4%)
    pallas_call x1, Pallas kernels, shards(): pl.pallas_call(functools.partial(kernel, (ndp, nrow, nlon), hops, scale),...  80 us
    unnamed x2, local copies, waits for them, and re-layouts  3.62 us

profile of v2, /device:TPU:1, one launch (start us, length us, event | category | flops | bytes accessed | tf_op | source)
XLA Modules:
  0.0 84.3 jit_solution(2858887739863258801)
XLA Ops:
  0.6 80.0 %shard_map.77 = (bf16[1,6,36,2048]{3,2,1,0:T(8,128)(2,1)}, f32[2,32,32]{2,1,0:T(8,128)}) custom-call(bf16[1,6,36,2048]{3,2,1,0:T(8,128)(2,1)} %x_hbm.1, bf16[3,3,2,2048]{3,2,1,0:T(2,128)(2,1)} %bitcast.3, bf16[2,2048,256]{2,1,0:T(8,128)(2,1)} %pw_hbm.1, bf16[512,256]{1,0:T(8,128)(2,1)} %proj_hbm.1, bf16[3,256]{1,0:T(4,128)(2,1)} %bitcast.5, s32[6,1,36]{2,1,0:T(1,128)} %bitcast.4), custom_call_target="tpu_custom_call" | custom-call | flops 13589544960 | bytes 3932160 | tf_op jit(solution)/shard_map/pallas_call | solution.py:613
  80.6 2.2 %copy.10 = bf16[1,6,36,2048]{3,2,1,0:T(8,128)(2,1)} copy(bf16[1,6,36,2048]{3,2,1,0:T(8,128)(2,1)} %get-tuple-element.4) | data formatting | bytes 1769472
  82.9 1.4 %copy.11 = f32[2,32,32]{2,1,0:T(8,128)} copy(f32[2,32,32]{2,1,0:T(8,128)} %get-tuple-element.5) | data formatting | bytes 16384

commit v3 on v2

--- a/solution.py
+++ b/solution.py
@@ -90,6 +90,9 @@
         other = (member + k) % (2 * nlon)
         return {"row": z * 2 + other // nlon, "lon": other % nlon}
 
+    def far_first(step, count):
+        return count // 2 + (step + 1) // 2 * (1 - 2 * (step % 2))
+
     started = []
 
     def remote(src, dst, ssem, rsem, device):
@@ -107,7 +110,7 @@
     loads = [
         pltpu.make_async_copy(src, dst, in_sem.at[n])
         for n, (src, dst) in enumerate((
-            (k_hbm, k_ref), (x_hbm.at[0], x_ref), (pw_hbm, pw_ref),
+            (k_hbm, k_ref), (x_hbm.at[0], x_ref), (pw_hbm.at[1], pw_ref.at[1]), (pw_hbm.at[0], pw_ref.at[0]),
             (proj_hbm, proj_ref), (cls_hbm, cls_ref), (lab_hbm, lab_ref),
         ))
     ]
@@ -205,10 +208,11 @@
         )
 
     outer_sides(0)
-    outer_sides(2)
     pl.semaphore_wait(barrier, len(peers))
     outer_send(0, 0)
+    outer_sides(2)
     outer_send(2, 0)
+    loads[3].wait()
     inner_taps(0)
     inner_taps(2)
     for g in (1, 2):
@@ -228,7 +232,7 @@
         if g == 0:
             cacc_ref[4] = tap(1, 1, 1)
 
-    for load in loads[3:]:
+    for load in loads[4:]:
         load.wait()
     ls_ref[...] = jnp.zeros_like(ls_ref)
     for r in range(rows):
@@ -305,13 +309,14 @@
             for e, (dst, device) in enumerate(((slice(g, g + 1), right), (slice(6 + g, 7 + g), left)))
         ]
 
+    order = (((0, 0), (1, 0)), ((0, 1),), ((0, 2), (1, 1), (1, 2)))
     for g in range(3):
         grads = head(g)
         g0_ref[1, 1 + g] = grads[0]
         g1_ref[1, 3 + g] = grads[1]
-        for b in (0, 1):
+        for b, at in order[g]:
             for i in (0, 2):
-                rows_back(b, i, g)
+                rows_back(b, i, at)
         inner_side(1, g)
         outer_side(1, g)
 
@@ -326,6 +331,8 @@
             keep = inside(row - hops[b] * (i - 1)).astype(F32)
             kf_ref[first : first + 3, :] = kf_ref[first : first + 3, :] * keep
 
+    dp_order = [far_first(s, ndp) for s in range(ndp - 1)]
+    z_order = [far_first(s, nz) for s in range(nz - 1)]
     zc = channels // nz
     hc = zc // 2
     half_rows = outc // ndp // 2
@@ -352,49 +359,70 @@
             ss_zb.at[b * nz + k], rs_zb.at[b * nz + k], z_device(k),
         )
 
-    def point_terms(b, taps, first, last, steps=(0, None)):
+    def point_tile(b, taps, first, cols):
+        terms = dot(gt_ref[: len(taps)].reshape(len(taps) * outc, pix_pad), xg_ref[:, cols])
+        total = None if first else tacc_ref[b, :, cols]
+        for slot, (i, j) in enumerate(taps):
+            t = b * 9 + i * 3 + j
+            term = terms[slot * outc : (slot + 1) * outc] * kf_ref[t : t + 1, cols]
+            total = term if total is None else total + term
+        return total
+
+    def point_terms(b, taps, first):
+        for slot, (i, j) in enumerate(taps):
+            turned(b, i, j, slot)
+
+        def step(n, carry):
+            cols = pl.ds(pl.multiple_of(n * zc, zc), zc)
+            tacc_ref[b, :, cols] = point_tile(b, taps, first, cols)
+            return carry
+
+        lax.fori_loop(0, nz, step, 0)
+
+    def point_last(b, taps):
+        for slot, (i, j) in enumerate(taps):
+            turned(b, i, j, slot)
+
         def step(s, carry):
-            k = (s + 1) % nz
-            cols = z_cols(k)
-            terms = dot(gt_ref[: len(taps)].reshape(len(taps) * outc, pix_pad), xg_ref[:, cols])
-            total = None if first else tacc_ref[:, cols]
-            for slot, (i, j) in enumerate(taps):
-                t = b * 9 + i * 3 + j
-                term = terms[slot * outc : (slot + 1) * outc] * kf_ref[t : t + 1, cols]
-                total = term if total is None else total + term
-            if not last:
-                tacc_ref[:, cols] = total
-            else:
-                block = total.astype(BF16).reshape(ndp, 2, half_rows, zc)
-                for c in (0, 1):
-                    t_ref[b, z_peer(k), c] = block[:, c]
-                core_copy(b, k).start()
+            k = far_first(s, nz)
+            block = point_tile(b, taps, False, z_cols(k)).astype(BF16).reshape(ndp, 2, half_rows, zc)
+            for c in (0, 1):
+                t_ref[b, z_peer(k), c] = block[:, c]
+            core_copy(b, k).start()
             return carry
 
-        lax.fori_loop(steps[0], nz if steps[1] is None else steps[1], step, 0)
+        lax.fori_loop(0, nz, step, 0)
 
     def chip_sums(b):
-        def add(k):
+        def add(k, slot):
             core_copy(b, k).wait_recv()
             n = z_peer(k)
             total = (t_ref[b, n, core].astype(F32) + rc_ref[b, n].astype(F32)).astype(BF16)
             sb_ref[b, n] = total[:, :, hc:]
-            sa_ref[b, :, n] = total[:, :, :hc]
+            sa_ref[b, :, slot] = total[:, :, :hc]
 
         def step(s, carry):
-            add(s + 1)
-            zb_copy(b, s + 1).start()
+            k = far_first(s, nz)
+            add(k, s)
+            zb_copy(b, k).start()
             return carry
 
-        lax.fori_loop(0, nz - 1, step, 0)
-        add(0)
-        return [
-            (k, send(
-                sa_ref.at[b, dp_peer(k)], rya_ref.at[b, k],
-                ss_ya.at[b * ndp + k], rs_ya.at[b * ndp + k], {"dp": dp_peer(k)},
-            ))
-            for k in range(1, ndp)
-        ]
+        def to_dp(part):
+            here = slice(0, nz // 2) if part == 0 else slice(nz // 2, nz)
+            return [
+                (k, send(
+                    sa_ref.at[b, dp_peer(k), here], rya_ref.at[b, k, here],
+                    ss_ya.at[(2 * b + part) * ndp + k], rs_ya.at[(2 * b + part) * ndp + k],
+                    {"dp": dp_peer(k)},
+                ))
+                for k in dp_order
+            ]
+
+        lax.fori_loop(0, nz // 2, step, 0)
+        ya = to_dp(0)
+        lax.fori_loop(nz // 2, nz - 1, step, 0)
+        add(0, nz - 1)
+        return ya + to_dp(1)
 
     def collect(copies, own, buffer):
         total = own.astype(F32)
@@ -404,13 +432,18 @@
         return total
 
     def second(b, ya):
-        ua_ref[b] = collect(ya, sa_ref[b, y], rya_ref.at[b]).astype(BF16)
+        for _, copy in ya:
+            copy.wait_recv()
+        total = sa_ref[b, y].astype(F32)
+        for k in range(1, ndp):
+            total = total + rya_ref[b, k].astype(F32)
+        ua_ref[b] = total.astype(BF16)
         za = [
             (k, send(
-                ua_ref.at[b, z_peer(k)], rza_ref.at[b, k],
+                ua_ref.at[b, s], rza_ref.at[b, k],
                 ss_za.at[b * nz + k], rs_za.at[b * nz + k], z_device(k),
             ))
-            for k in range(1, nz)
+            for s, k in enumerate(z_order)
         ]
         zb = [(k, zb_copy(b, k)) for k in range(1, nz)]
         ub_ref[b] = collect(zb, sb_ref[b, z], rzb_ref.at[b]).astype(BF16)
@@ -419,12 +452,12 @@
                 ub_ref.at[b, dp_peer(k)], ryb_ref.at[b, k],
                 ss_yb.at[b * ndp + k], rs_yb.at[b * ndp + k], {"dp": dp_peer(k)},
             ))
-            for k in range(1, ndp)
+            for k in dp_order
         ]
         return za, yb
 
     def third(b, za, yb):
-        part_a = collect(za, ua_ref[b, z], rza_ref.at[b])
+        part_a = collect(za, ua_ref[b, nz - 1], rza_ref.at[b])
         part_b = collect(yb, ub_ref[b, y], ryb_ref.at[b])
         v_ref[b] = jnp.concatenate([part_a, part_b], axis=1).astype(BF16)
         return [
@@ -462,40 +495,34 @@
 
         lax.fori_loop(0, nz, step, 0)
 
+    across = [(1, j) for j in range(3)]
+    middle = [(0, 1), (2, 1)]
+    sides = [(i, j) for i in (0, 2) for j in (0, 2)]
+
+    def arrived(b, i):
+        for g in (range(3) if b == 1 else (0, 2)):
+            for copy in g_copies[b, i, g]:
+                copy.wait_recv()
+
     pass_on(0, 0)
     pass_on(1, 0)
-    for g in range(3):
-        for copy in g_copies[1, 1, g]:
-            copy.wait_recv()
-    for j in range(3):
-        turned(1, 1, j, j)
-    point_terms(1, [(1, j) for j in range(3)], True, False)
     pass_on(0, 1)
+    arrived(0, 1)
+    point_terms(0, across, True)
+    pass_on(0, 2)
+    point_terms(0, middle, False)
+    arrived(1, 1)
+    point_terms(1, across, True)
     pass_on(1, 1)
-    pass_on(0, 2)
-    for i in range(3):
-        for g in (0, 2):
-            for copy in g_copies[0, i, g]:
-                copy.wait_recv()
-        for j in range(3):
-            turned(0, i, j, 3 * i + j)
-    inner = [(i, j) for i in range(3) for j in range(3)]
-    point_terms(0, inner, True, True, (0, nz // 2))
+    arrived(0, 0)
+    arrived(0, 2)
+    point_last(0, sides)
     pass_on(1, 2)
-    point_terms(0, inner, True, True, (nz // 2, nz))
     ya0 = chip_sums(0)
-    middle = [(0, 1), (2, 1)]
-    for slot, (i, j) in enumerate(middle):
-        turned(1, i, j, slot)
-    point_terms(1, middle, False, False)
-    sides = [(i, j) for i in (0, 2) for j in (0, 2)]
-    for i in (0, 2):
-        for g in range(3):
-            for copy in g_copies[1, i, g]:
-                copy.wait_recv()
-    for slot, (i, j) in enumerate(sides):
-        turned(1, i, j, slot)
-    point_terms(1, sides, False, True)
+    point_terms(1, middle, False)
+    arrived(1, 0)
+    arrived(1, 2)
+    point_last(1, sides)
     ya1 = chip_sums(1)
     input_terms(0)
     za0, yb0 = second(0, ya0)
@@ -573,7 +600,7 @@
         pltpu.VMEM(classes.shape, BF16),
         pltpu.VMEM(label_rows.shape, jnp.int32),
         pltpu.VMEM(features.shape[1:], BF16),
-        dma(6), pltpu.SemaphoreType.DMA,
+        dma(7), pltpu.SemaphoreType.DMA,
         pltpu.VMEM((rows, pitch, channels), BF16),
         pltpu.VMEM((pix_pad, channels), BF16),
         pltpu.VMEM((rows * pitch, pix_pad), BF16),
@@ -593,7 +620,7 @@
         pltpu.VMEM((3, 9, gp, outc), BF16),
         pltpu.VMEM((9, outc, pix_pad), BF16),
         pltpu.VMEM((pix, channels), F32),
-        pltpu.VMEM((outc, channels), F32),
+        pltpu.VMEM((2, outc, channels), F32),
         pltpu.VMEM((2, nz, 2, ndp, half, zc), BF16),
         pltpu.VMEM((2, nz, ndp, half, zc), BF16),
         pltpu.VMEM((2, ndp, nz, half, hc), BF16),
@@ -607,7 +634,7 @@
         pltpu.VMEM((2, half, zc), BF16),
         pltpu.VMEM((2, 2 * nlon, half, zc), BF16),
         dma(24), dma(24), dma(12), dma(12), dma(12), dma(12), dma(24), dma(24),
-        dma(2 * nz), dma(2 * nz), dma(2 * ndp), dma(2 * ndp), dma(2 * nz), dma(2 * nz),
+        dma(2 * nz), dma(2 * nz), dma(4 * ndp), dma(4 * ndp), dma(2 * nz), dma(2 * nz),
         dma(2 * nz), dma(2 * nz), dma(2 * ndp), dma(2 * ndp), dma(4 * nlon), dma(4 * nlon),
     ]
     return pl.pallas_call(

time: 84.5 us -> 83.9 us (level)
  no operation moved by 1% of the time
where the time goes in v3:
time: 83.9 us; the launch traced here: 83.6 us
  Pallas kernels  79.4 us (95%)
  local copies, waits for them, and re-layouts  3.62 us (4%)
    pallas_call x1, Pallas kernels, shards(): pl.pallas_call(functools.partial(kernel, (ndp, nrow, nlon), hops, scale),...  79.4 us
    unnamed x2, local copies, waits for them, and re-layouts  3.62 us

profile of v3, /device:TPU:1, one launch (start us, length us, event | category | flops | bytes accessed | tf_op | source)
XLA Modules:
  0.0 83.6 jit_solution(2080398511249972064)
XLA Ops:
  0.6 79.4 %shard_map.77 = (bf16[1,6,36,2048]{3,2,1,0:T(8,128)(2,1)}, f32[2,32,32]{2,1,0:T(8,128)}) custom-call(bf16[1,6,36,2048]{3,2,1,0:T(8,128)(2,1)} %x_hbm.1, bf16[3,3,2,2048]{3,2,1,0:T(2,128)(2,1)} %bitcast.3, bf16[2,2048,256]{2,1,0:T(8,128)(2,1)} %pw_hbm.1, bf16[512,256]{1,0:T(8,128)(2,1)} %proj_hbm.1, bf16[3,256]{1,0:T(4,128)(2,1)} %bitcast.5, s32[6,1,36]{2,1,0:T(1,128)} %bitcast.4), custom_call_target="tpu_custom_call" | custom-call | flops 13589544960 | bytes 3932160 | tf_op jit(solution)/shard_map/pallas_call | solution.py:640
  80.0 2.2 %copy.10 = bf16[1,6,36,2048]{3,2,1,0:T(8,128)(2,1)} copy(bf16[1,6,36,2048]{3,2,1,0:T(8,128)(2,1)} %get-tuple-element.4) | data formatting | bytes 1769472
  82.3 1.4 %copy.11 = f32[2,32,32]{2,1,0:T(8,128)} copy(f32[2,32,32]{2,1,0:T(8,128)} %get-tuple-element.5) | data formatting | bytes 16384
